TPU v7x, 128 devices: a whole 4x4x4 slice. The times are simulated.
128 devices in a mesh: sq: 8 (over z, core), sk: 16 (over y, x).
Axes of the slice: x: 4, y: 4, z: 4, core: 2. Of those that a mesh axis runs over, the one named last changes fastest.
Arguments:
- queries: bfloat16 [2048, 128, 576], P('sk', 'sq'), may hold values from -40 to 40
- out_grad: bfloat16 [2048, 128, 512], P('sk', 'sq'), may hold values from -24 to 24
- latent_keys: bfloat16 [256, 128, 576], P('sk'), may hold values from -6 to 6
- index_queries: bfloat16 [2048, 64, 128], P('sk', 'sq'), may hold values from -7 to 7
- index_weights: float32 [2048, 64], P('sk', 'sq'), may hold values from 1 to 16
- index_keys: bfloat16 [256, 128, 128], P('sk'), may hold values from -6 to 6
- picks: int32 [16, 16], replicated, may hold values from 0 to 255, as said below
Outputs:
- query_grad: bfloat16 [2048, 128, 576], P('sk', 'sq')
- latent_key_grad: float32 [256, 128, 576], P('sk', 'sq')
- index_query_grad: float32 [2048, 64, 128], P('sk', 'sq')
- index_weight_grad: float32 [2048, 64], P('sk', 'sq')
- index_key_grad: float32 [256, 128, 128], P('sk', 'sq')
Inputs may be any that keep to these rules, and one draw needn't show every extreme that they name: `picks`: row t lists 16 distinct key blocks for the queries of tile t. Within a row at most 2 blocks fall in one aligned range of 16 consecutive blocks, and every row has a range that holds exactly 2 of them.
All inputs are finite; a program needn't handle non-finite values.
Results may differ from a plain program's by a relative error of at most 0.0045.
Values may be sent and summed in bfloat16 or wider, within the bound.
A program may use at most 192 MiB of HBM per device.

v0:
```python
import math

import jax
import jax.numpy as jnp
from jax import lax
from jax.sharding import PartitionSpec as P

H = 128
HI = 64
ID = 128
CAP = 2


ATTN_SCALE = 0.1353


def pack_blocks(source, send_block, send_valid):
    gathered = jnp.take(source, send_block, axis=0)
    return jnp.where(send_valid[:, :, None, None], gathered, jnp.zeros_like(gathered))


def densify(onehot, received):
    flat_rows = received.reshape(
        received.shape[0] * received.shape[1], received.shape[2], received.shape[3]
    )
    return jnp.einsum("sn,nrd->srd", onehot, flat_rows, precision=lax.Precision.HIGHEST)


def body(queries, out_grad, latent_keys, index_queries, index_weights, index_keys, picks):
    sk_count = lax.axis_size("sk")
    my_column = lax.axis_index("sk")
    block_count = latent_keys.shape[0]
    block_rows = latent_keys.shape[1]
    key_width = latent_keys.shape[2]
    index_width = index_keys.shape[2]
    pick_count = picks.shape[1]
    latent_width = out_grad.shape[2]
    owner_of = picks // block_count
    local_block = picks % block_count
    positions = jnp.arange(pick_count, dtype=jnp.int32)
    same_owner = owner_of[:, :, None] == owner_of[:, None, :]
    earlier = positions[None, :] < positions[:, None]
    rank_among = jnp.sum(same_owner & earlier[None, :, :], axis=2)
    slot_ids = jnp.arange(CAP, dtype=jnp.int32)
    matches = (owner_of[:, None, :] == my_column) & (
        rank_among[:, None, :] == slot_ids[None, :, None]
    )
    send_block = jnp.sum(jnp.where(matches, local_block[:, None, :], 0), axis=2)
    send_valid = jnp.any(matches, axis=2)
    my_owner = jnp.take(owner_of, my_column, axis=0)
    my_rank = jnp.take(rank_among, my_column, axis=0)
    slot_of_pick = my_owner * CAP + my_rank
    slot_total = sk_count * CAP
    latent_recv, index_recv = (
        lax.all_to_all(
            pack_blocks(latent_keys, send_block, send_valid),
            "sk",
            split_axis=0,
            concat_axis=0,
            tiled=True,
        ),
        lax.all_to_all(
            pack_blocks(index_keys, send_block, send_valid),
            "sk",
            split_axis=0,
            concat_axis=0,
            tiled=True,
        ),
    )
    latent_pick = jnp.take(
        latent_recv.reshape(slot_total, block_rows, key_width), slot_of_pick, axis=0
    )
    latent_pick = latent_pick.reshape(pick_count * block_rows, key_width)
    index_pick = jnp.take(
        index_recv.reshape(slot_total, block_rows, index_width), slot_of_pick, axis=0
    )
    index_pick = index_pick.reshape(pick_count * block_rows, index_width)
    scores = ATTN_SCALE * jnp.einsum(
        "qhd,kd->qhk", queries, latent_pick, preferred_element_type=jnp.float32
    )
    attn_probs = jax.nn.softmax(scores, axis=-1)
    dprobs = jnp.einsum(
        "qhv,kv->qhk", out_grad, latent_pick[:, :latent_width], preferred_element_type=jnp.float32
    )
    rowdot = jnp.sum(attn_probs * dprobs, axis=-1, keepdims=True)
    dscore = (attn_probs * (dprobs - rowdot)).astype(jnp.bfloat16)
    query_grad = (
        ATTN_SCALE
        * jnp.einsum("qhk,kd->qhd", dscore, latent_pick, preferred_element_type=jnp.float32)
    ).astype(jnp.bfloat16)
    key_part = ATTN_SCALE * jnp.einsum(
        "qhk,qhd->kd", dscore, queries, preferred_element_type=jnp.float32
    )
    value_part = jnp.einsum(
        "qhk,qhv->kv", attn_probs.astype(jnp.bfloat16), out_grad, preferred_element_type=jnp.float32
    )
    key_part = key_part + jnp.pad(value_part, ((0, 0), (0, key_width - latent_width)))
    head_mass = jnp.sum(attn_probs, axis=1)
    index_scale = 1.0 / math.sqrt(ID * HI)
    index_sim = jnp.einsum(
        "qjd,kd->qjk", index_queries, index_pick, preferred_element_type=jnp.float32
    )
    active = jnp.maximum(index_sim, 0.0)
    partial_logit = index_scale * jnp.sum(index_weights[:, :, None] * active, axis=1)
    logits, mass_total = lax.psum((partial_logit, head_mass), "sq")
    target = mass_total / H
    dlogit = jax.nn.softmax(logits, axis=-1) - target
    index_dsim = jnp.where(
        index_sim > 0, index_scale * dlogit[:, None, :] * index_weights[:, :, None], 0.0
    ).astype(jnp.bfloat16)
    index_query_grad = jnp.einsum(
        "qjk,kd->qjd", index_dsim, index_pick, preferred_element_type=jnp.float32
    )
    index_weight_grad = index_scale * jnp.sum(dlogit[:, None, :] * active, axis=2)
    index_part = jnp.einsum(
        "qjk,qjd->kd", index_dsim, index_queries, preferred_element_type=jnp.float32
    )
    onehot = (
        (send_block.reshape(-1)[None, :] == jnp.arange(block_count, dtype=jnp.int32)[:, None])
        & send_valid.reshape(-1)[None, :]
    ).astype(jnp.float32)
    latent_picked = key_part.reshape(pick_count, block_rows, key_width)
    index_picked = index_part.reshape(pick_count, block_rows, index_width)
    latent_slots = (
        jnp.zeros((slot_total, block_rows, key_width), jnp.float32)
        .at[slot_of_pick]
        .set(latent_picked)
        .reshape(sk_count, CAP, block_rows, key_width)
    )
    index_slots = (
        jnp.zeros((slot_total, block_rows, index_width), jnp.float32)
        .at[slot_of_pick]
        .set(index_picked)
        .reshape(sk_count, CAP, block_rows, index_width)
    )
    got_latent, got_index = (
        lax.all_to_all(latent_slots, "sk", split_axis=0, concat_axis=0, tiled=True),
        lax.all_to_all(index_slots, "sk", split_axis=0, concat_axis=0, tiled=True),
    )
    latent_key_grad, index_key_grad = (
        lax.psum_scatter(densify(onehot, got_latent), "sq", scatter_dimension=1, tiled=True),
        lax.psum_scatter(densify(onehot, got_index), "sq", scatter_dimension=1, tiled=True),
    )
    return (query_grad, latent_key_grad, index_query_grad, index_weight_grad, index_key_grad)


def solution(mesh):
    placed = (
        P("sk", "sq", None),
        P("sk", "sq", None),
        P("sk", None, None),
        P("sk", "sq", None),
        P("sk", "sq"),
        P("sk", None, None),
        P(),
    )
    return jax.shard_map(
        body,
        mesh=mesh,
        in_specs=placed,
        out_specs=(
            P("sk", "sq", None),
            P("sk", "sq", None),
            P("sk", "sq", None),
            P("sk", "sq"),
            P("sk", "sq", None),
        ),
        check_vma=False,
    )
```

profile of v0, /device:TPU:0, one launch (start us, length us, event | category | flops | bytes accessed | tf_op | source)
XLA Modules:
  0.0 539.2 jit_solution(10667428274624823947)
XLA Ops:
  10.0 1.8 gather_fusion.2
  11.8 1.2 select_select_fusion.1
  12.9 7.1 %all-to-all-start.2 = ((bf16[16,2,128,128]{3,2,1,0:T(8,128)(2,1)}), bf16[16,2,128,128]{3,2,1,0:T(8,128)(2,1)S(1)}, u32[]{:S(2)}, u32[]{:S(2)}) async-start(bf16[16,2,128,128]{3,2,1,0:T(8,128)(2,1)} %select_select_fusion.1), calls=%async_computation.3 | async-start | bytes 2097152 | tf_op jit(solution)/shard_map/all_to_all | solution.py:62
  20.1 5.0 gather_fusion
  25.1 5.0 select_select_fusion
  30.1 7.6 %all-to-all-done.2 = bf16[16,2,128,128]{3,2,1,0:T(8,128)(2,1)S(1)} async-done(((bf16[16,2,128,128]{3,2,1,0:T(8,128)(2,1)}), bf16[16,2,128,128]{3,2,1,0:T(8,128)(2,1)S(1)}, u32[]{:S(2)}, u32[]{:S(2)}) %all-to-all-start.2) | async-done | bytes 1048608 | tf_op jit(solution)/shard_map/all_to_all | solution.py:62
  37.7 4.6 all-to-all-start
  42.5 4.5 copy.82
  47.2 1.4 gather_fusion.3
  48.6 1.4 bitcast_select_fusion.1
  50.7 5.5 %fusion.9 = (f32[128,2048]{0,1:T(8,128)S(1)}, f32[2048,128,8]{1,0,2:T(8,128)}) fusion(f32[128,8]{0,1:T(8,128)S(1)} %copy-done.6, bf16[128,8,128]{2,1,0:T(8,128)(2,1)} %param.12, bf16[2048,128]{1,0:T(8,128)(2,1)S(1)} %bitcast_select_fusion.1), kind=kOutput, calls=%fused_computation.19 | convolution fusion | flops 542900224 | bytes 10227712 | tf_op jit(solution)/shard_map/qjd,kd->qjk/dot_general | solution.py:100
  57.3 51.5 %all-to-all-done = bf16[16,2,128,576]{2,3,1,0:T(8,128)(2,1)} async-done(((bf16[16,2,128,576]{2,3,1,0:T(8,128)(2,1)}), bf16[16,2,128,576]{2,3,1,0:T(8,128)(2,1)}, u32[]{:S(2)}, u32[]{:S(2)}) %all-to-all-start) | async-done | bytes 4718624 | tf_op jit(solution)/shard_map/all_to_all | solution.py:55
  108.8 4.6 gather_fusion.1
  113.4 4.3 copy.73
  117.7 2.0 bitcast_select_fusion
  119.7 9.5 %fusion.21 = f32[2048,128,16]{1,0,2:T(8,128)} fusion(bf16[128,16,576]{0,2,1:T(8,128)(2,1)S(1)} %copy-done, bf16[2048,576]{1,0:T(8,128)(2,1)S(1)} %bitcast_select_fusion), kind=kOutput, calls=%fused_computation.35 | convolution fusion | flops 4831838208 | bytes 21495808 | tf_op jit(solution)/shard_map/qhd,kd->qhk/dot_general | solution.py:78
  129.2 17.9 %fusion.60 = (f32[128,16]{0,1:T(8,128)S(1)}, f32[128,16,2048]{0,2,1:T(8,128)}) fusion(f32[2048,128,16]{1,0,2:T(8,128)} %fusion.21), kind=kOutput, calls=%fused_computation.97 | output fusion | flops 16779264 | bytes 33562624 | tf_op jit(solution)/shard_map/sub | solution.py:81
  147.1 13.5 %fusion.55 = (f32[128,2048]{0,1:T(8,128)}, f32[128,16]{0,1:T(8,128)S(1)}, f32[2048,128,16]{1,0,2:T(8,128)}) fusion(f32[128,16,2048]{0,2,1:T(8,128)} %get-tuple-element.48, f32[128,16]{0,1:T(8,128)S(1)} %get-tuple-element.47, bf16[128,16,512]{0,2,1:T(8,128)(2,1)} %copy.82, bf16[2048,576]{1,0:T(8,128)(2,1)S(1)} %bitcast_select_fusion), kind=kOutput, calls=%fused_computation.96 | convolution fusion | flops 4311480320 | bytes 38813696 | tf_op jit(solution)/shard_map/qhv,kv->qhk/dot_general | solution.py:82
  160.6 15.0 %fusion.3 = bf16[128,16,2048]{0,2,1:T(8,128)(2,1)} fusion(f32[2048,128,16]{1,0,2:T(8,128)} %get-tuple-element.49, f32[128,16]{0,1:T(8,128)S(1)} %get-tuple-element.38, f32[128,16,2048]{0,2,1:T(8,128)} %get-tuple-element.48, f32[128,16]{0,1:T(8,128)S(1)} %get-tuple-element.47), kind=kLoop, calls=%fused_computation.11 | loop fusion | flops 16777216 | bytes 41959424 | tf_op jit(solution)/shard_map/convert_element_type | solution.py:86
  175.6 51.0 %all-reduce.4.cloned.1.call-done = (f32[128,2048]{0,1:T(8,128)}, f32[128,2048]{0,1:T(8,128)}) async-done(((f32[128,2048]{0,1:T(8,128)}, f32[128,2048]{0,1:T(8,128)}), (f32[128,2048]{0,1:T(8,128)}, f32[128,2048]{0,1:T(8,128)})) %all-reduce.4.cloned.1.call-update) | async-done | bytes 2097168 | tf_op jit(solution)/shard_map/psum | solution.py:105
  226.6 1.5 reduce_max.19
  228.1 1.5 fusion.26
  229.6 1.8 broadcast_multiply_fusion
  232.4 5.6 %fusion.31 = f32[2048,128,1]{1,0,2:T(8,128)} fusion(bf16[128,8,128]{2,1,0:T(8,128)(2,1)} %param.12, f32[2048,128,8]{1,0,2:T(8,128)} %get-tuple-element.51, f32[128,2048]{0,1:T(8,128)S(1)} %get-tuple-element.41, f32[128,8]{0,1:T(8,128)S(1)} %copy-done.6), kind=kOutput, calls=%fused_computation.51 | convolution fusion | flops 545259520 | bytes 10752000 | tf_op jit(solution)/shard_map/qjk,qjd->kd/dot_general | solution.py:115
  238.0 1.6 broadcast_in_dim.135
  239.6 3.6 scatter_fusion.1
  243.2 4.6 copy.92
  247.7 6.9 %all-to-all-start.3 = ((f32[16,2,128,128]{3,1,2,0:T(2,128)}), f32[16,2,128,128]{3,1,2,0:T(2,128)}, u32[]{:S(2)}, u32[]{:S(2)}) async-start(f32[16,2,128,128]{3,1,2,0:T(2,128)} %copy.92), calls=%async_computation.4 | async-start | bytes 4194304 | tf_op jit(solution)/shard_map/all_to_all | solution.py:138
  254.6 19.1 %fusion.16 = f32[2048,512]{0,1:T(8,128)} fusion(bf16[128,16,512]{0,2,1:T(8,128)(2,1)} %copy.82, f32[128,16]{0,1:T(8,128)S(1)} %get-tuple-element.47, f32[2048,128,16]{1,0,2:T(8,128)} %fusion.21), kind=kOutput, calls=%fused_computation.32 | convolution fusion | flops 4315942912 | bytes 23076864 | tf_op jit(solution)/shard_map/qhk,qhv->kv/dot_general | solution.py:94
  273.7 8.2 %fusion.15 = f32[72,16,8,128]{3,2,1,0:T(8,128)S(1)} fusion(f32[2048,512]{0,1:T(8,128)} %fusion.16, bf16[128,16,2048]{0,2,1:T(8,128)(2,1)} %fusion.3, bf16[128,16,576]{0,2,1:T(8,128)(2,1)S(1)} %copy-done), kind=kOutput, calls=%fused_computation.29 | convolution fusion | flops 4834197504 | bytes 19660800 | tf_op jit(solution)/shard_map/qhk,qhd->kd/dot_general | solution.py:91
  281.9 2.6 copy.115
  284.5 4.8 broadcast_in_dim.128
  289.2 8.5 %scatter_fusion = f32[32,128,576]{1,2,0:T(8,128)} fusion(f32[32,128,576]{1,2,0:T(8,128)} %broadcast_in_dim.128, s32[16]{0:T(128)S(1)} %get-tuple-element.44, f32[16,128,576]{1,2,0:T(8,128)} %bitcast.123), kind=kCustom, calls=%fused_computation.4 | custom fusion | bytes 14155840 | tf_op jit(solution)/shard_map/scatter | solution.py:127
  297.7 17.1 %copy.84 = f32[16,2,128,576]{2,1,3,0:T(2,128)} copy(f32[16,2,128,576]{2,3,1,0:T(8,128)} %bitcast.121) | data formatting | bytes 18874368 | tf_op jit(solution)/shard_map/reshape | solution.py:128
  314.8 7.3 %all-to-all-start.1 = ((f32[16,2,128,576]{2,1,3,0:T(2,128)}), f32[16,2,128,576]{2,1,3,0:T(2,128)}, u32[]{:S(2)}, u32[]{:S(2)}) async-start(f32[16,2,128,576]{2,1,3,0:T(2,128)} %copy.84), calls=%async_computation.1 | async-start | bytes 18874368 | tf_op jit(solution)/shard_map/all_to_all | solution.py:137
  322.7 2.8 copy.93
  325.5 1.9 fusion.39
  327.5 129.1 %all-to-all-done.1 = f32[16,2,128,576]{2,1,3,0:T(2,128)} async-done(((f32[16,2,128,576]{2,1,3,0:T(2,128)}), f32[16,2,128,576]{2,1,3,0:T(2,128)}, u32[]{:S(2)}, u32[]{:S(2)}) %all-to-all-start.1) | async-done | bytes 9437216 | tf_op jit(solution)/shard_map/all_to_all | solution.py:137
  456.6 9.2 %copy.85 = f32[16,2,128,576]{2,1,0,3:T(2,128)} copy(f32[16,2,128,576]{2,1,3,0:T(2,128)} %all-to-all-done.1) | data formatting | bytes 18874368 | tf_op jit(solution)/shard_map/all_to_all | solution.py:137
  465.7 12.1 %copy.102 = f32[32,128,576]{2,0,1:T(8,128)} copy(f32[32,128,576]{1,0,2:T(8,128)} %bitcast.122) | data formatting | bytes 18874368 | tf_op jit(solution)/shard_map/reshape | solution.py:23
  477.8 7.8 %fusion.41 = f32[16,128,576]{2,0,1:T(8,128)} fusion(f32[32,128,576]{2,0,1:T(8,128)} %copy.102, s32[32]{0:T(128)S(1)} %eq.58, pred[32]{0:T(512)(128)(4,1)S(1)} %and.64), kind=kOutput, calls=%fused_computation.71 | convolution fusion | flops 452985856 | bytes 14155936 | tf_op jit(solution)/shard_map/sn,nrd->srd/dot_general | solution.py:26
  485.7 9.5 %multiply_convert_fusion = bf16[128,16,576]{0,2,1:T(8,128)(2,1)} fusion(bf16[128,16,2048]{0,2,1:T(8,128)(2,1)} %fusion.3, bf16[2048,576]{1,0:T(8,128)(2,1)} %copy-done.1), kind=kOutput, calls=%fused_computation.30 | convolution fusion | flops 4834197504 | bytes 13107200 | tf_op jit(solution)/shard_map/qhk,kd->qhd/dot_general | solution.py:89
  495.1 4.8 fusion.27
  499.9 1.1 copy.95
  501.0 4.2 fusion.10
  505.8 1.6 copy.96
  507.5 22.7 %reduce-scatter.3.cloned.1.call-done = f32[16,16,576]{2,0,1:T(8,128)} async-done(((f32[16,128,576]{2,0,1:T(8,128)}), f32[16,16,576]{2,0,1:T(8,128)}) %reduce-scatter.3.cloned.1.call-update) | async-done | bytes 589840 | tf_op jit(solution)/shard_map/reduce_scatter | solution.py:141
  530.1 2.1 copy.94
  (50 shorter events, 7.2 us)
Async XLA Ops:
  7.2 112.5 %copy-start = (bf16[128,16,576]{0,2,1:T(8,128)(2,1)S(1)}, bf16[128,16,576]{0,2,1:T(8,128)(2,1)}, u32[]{:S(2)}) copy-start(bf16[128,16,576]{0,2,1:T(8,128)(2,1)} %param.9) | copy-start | bytes 7077892
  9.3 0.6 copy-start.9
  10.0 15.1 %copy-start.7 = (pred[16,2]{1,0:T(8,128)(4,1)}, pred[16,2]{1,0:T(8,128)(4,1)S(1)}, u32[]{:S(2)}) copy-start(pred[16,2]{1,0:T(8,128)(4,1)S(1)} %copy.70) | copy-start | bytes 100
  12.9 24.8 %all-to-all-start.2 = ((bf16[16,2,128,128]{3,2,1,0:T(8,128)(2,1)}), bf16[16,2,128,128]{3,2,1,0:T(8,128)(2,1)S(1)}, u32[]{:S(2)}, u32[]{:S(2)}) async-start(bf16[16,2,128,128]{3,2,1,0:T(8,128)(2,1)} %select_select_fusion.1), calls=%async_computation.3 | async-start | bytes 2097152 | tf_op jit(solution)/shard_map/all_to_all | solution.py:62
  30.1 20.6 %copy-start.6 = (f32[128,8]{0,1:T(8,128)S(1)}, f32[128,8]{0,1:T(8,128)}, u32[]{:S(2)}) copy-start(f32[128,8]{0,1:T(8,128)} %param.13) | copy-start | bytes 12292
  37.7 71.0 %all-to-all-start = ((bf16[16,2,128,576]{2,3,1,0:T(8,128)(2,1)}), bf16[16,2,128,576]{2,3,1,0:T(8,128)(2,1)}, u32[]{:S(2)}, u32[]{:S(2)}) async-start(bf16[16,2,128,576]{2,3,1,0:T(8,128)(2,1)} %select_select_fusion), calls=%async_computation | async-start | bytes 9437184 | tf_op jit(solution)/shard_map/all_to_all | solution.py:55
  42.3 184.3 %all-reduce.4.cloned.1.call-start = ((), (), s32[]{:S(2)}) async-start(), calls=%async_computation.8 | async-start | bytes 4194304 | tf_op jit(solution)/shard_map/psum | solution.py:105
  49.9 0.8 copy-start.2
  119.7 27.4 %copy-start.1 = (bf16[2048,576]{1,0:T(8,128)(2,1)}, bf16[2048,576]{1,0:T(8,128)(2,1)S(1)}, u32[]{:S(2)}) copy-start(bf16[2048,576]{1,0:T(8,128)(2,1)S(1)} %bitcast_select_fusion) | copy-start | bytes 7077892
  231.4 1.0 copy-start.4
  247.7 67.0 %all-to-all-start.3 = ((f32[16,2,128,128]{3,1,2,0:T(2,128)}), f32[16,2,128,128]{3,1,2,0:T(2,128)}, u32[]{:S(2)}, u32[]{:S(2)}) async-start(f32[16,2,128,128]{3,1,2,0:T(2,128)} %copy.92), calls=%async_computation.4 | async-start | bytes 4194304 | tf_op jit(solution)/shard_map/all_to_all | solution.py:138
  314.8 7.7 %copy-start.10 = (s32[16,2]{0,1:T(2,128)S(1)}, s32[16,2]{0,1:T(2,128)}, u32[]{:S(2)}) copy-start(s32[16,2]{0,1:T(2,128)} %copy-done.9) | copy-start | bytes 388
  314.8 7.7 %copy-start.8 = (pred[16,2]{1,0:T(8,128)(4,1)S(1)}, pred[16,2]{1,0:T(8,128)(4,1)}, u32[]{:S(2)}) copy-start(pred[16,2]{1,0:T(8,128)(4,1)} %copy-done.7) | copy-start | bytes 100
  314.8 141.8 %all-to-all-start.1 = ((f32[16,2,128,576]{2,1,3,0:T(2,128)}), f32[16,2,128,576]{2,1,3,0:T(2,128)}, u32[]{:S(2)}, u32[]{:S(2)}) async-start(f32[16,2,128,576]{2,1,3,0:T(2,128)} %copy.84), calls=%async_computation.1 | async-start | bytes 18874368 | tf_op jit(solution)/shard_map/all_to_all | solution.py:137
  322.1 183.7 %reduce-scatter.5.cloned.1.call-start = ((), (), s32[]{:S(2)}) async-start(), calls=%async_computation.7 | async-start | bytes 1179648 | tf_op jit(solution)/shard_map/reduce_scatter | solution.py:142
  327.4 202.7 %reduce-scatter.3.cloned.1.call-start = ((), (), s32[]{:S(2)}) async-start(), calls=%async_computation.6 | async-start | bytes 5898240 | tf_op jit(solution)/shard_map/reduce_scatter | solution.py:141
  485.6 9.5 %copy-start.3 = (bf16[2048,128]{1,0:T(8,128)(2,1)S(1)}, bf16[2048,128]{1,0:T(8,128)(2,1)}, u32[]{:S(2)}) copy-start(bf16[2048,128]{1,0:T(8,128)(2,1)} %copy-done.2) | copy-start | bytes 1572868
  485.6 9.5 %copy-start.5 = (f32[128,2048]{0,1:T(8,128)S(1)}, f32[128,2048]{0,1:T(8,128)}, u32[]{:S(2)}) copy-start(f32[128,2048]{0,1:T(8,128)} %copy-done.4) | copy-start | bytes 3145732
Sparse Core Ops, SparseCore 0:
  160.7 65.8 all-reduce.3
  327.5 32.0 reduce-scatter.4
  485.8 44.3 reduce-scatter.2
where the time goes:
time: 543 us; the launch traced here: 539 us
  waiting for transfers between devices  262 us (48%)
  local copies, waits for them, and re-layouts  95.7 us (18%)
  matrix products  85.3 us (16%)
  other arithmetic  55.5 us (10%)
  starting transfers between devices  26.4 us (5%)
  between operations  14.4 us (3%)
    all_to_all x1, waiting for transfers between devices, body(): lax.all_to_all(latent_slots, 'sk', split_axis=0, concat_axis=0, tiled=True)  129 us
    all_to_all x1, waiting for transfers between devices, body(): lax.all_to_all(pack_blocks(latent_keys, send_block, send_valid), 'sk', sp...  51.5 us
    psum x1, waiting for transfers between devices, body(): logits, mass_total = lax.psum((partial_logit, head_mass), 'sq')  51 us
    reduce_scatter x1, waiting for transfers between devices, body(): lax.psum_scatter(densify(onehot, got_latent), 'sq', scatter_dimension=1,...  22.7 us
    dot_general x1, matrix products, body(): jnp.einsum('qhk,qhv->kv', attn_probs.astype(jnp.bfloat16), out_grad, pref...  19.1 us
    sub x1, other arithmetic, body(): attn_probs = jax.nn.softmax(scores, axis=-1)  17.9 us
    reshape x1, local copies, waits for them, and re-layouts, body(): latent_slots = jnp.zeros((slot_total, block_rows, key_width), jnp.float32...  17.1 us
    convert_element_type x1, other arithmetic, body(): dscore = (attn_probs * (dprobs - rowdot)).astype(jnp.bfloat16)  15 us
  transfers between devices with their start and end apart: 7, of which 5 were waited for; matrix products, arithmetic and copies ran while one was open for 29% of the time, Pallas kernels for 0%

commit v1 on v0

v1 whole, which is shorter than its diff:
```python
import math

import jax
import jax.numpy as jnp
from jax import lax
from jax.experimental import pallas as pl
from jax.experimental.pallas import tpu as pltpu
from jax.sharding import PartitionSpec as P

H = 128
HI = 64
ID = 128
CAP = 2
LAT = 512
KD = 576
ATTN_SCALE = 0.1353
INDEX_SCALE = 1.0 / math.sqrt(ID * HI)
LOG2E = 1.4426950408889634

MESH = pl.DeviceIdType.MESH
F32 = jnp.float32
BF16 = jnp.bfloat16

NK = 16
NS = 8
NZ = 4
SUB = 16
PICKS = 16
CH = PICKS * SUB
KEYS = NS * CH
ROWS = 2048
QT = 128
HL = 16
JL = 8
QL = 16
SLOT = CAP * SUB
W = 768
IO = 640
R = 256
KC = 256


def dot(a, b):
    return jnp.dot(a, b, preferred_element_type=F32)


def dot_nt(a, b):
    return lax.dot_general(a, b, (((1,), (1,)), ((), ())), preferred_element_type=F32)


def onehot(index, shape, axis):
    hit = lax.broadcasted_iota(jnp.int32, shape, axis) == index
    return jnp.where(hit, 1.0, 0.0).astype(BF16)


def kernel(
    q_hbm, do_hbm, lat_hbm, iq_hbm, iw_hbm, idx_hbm, slot_col, slot_row, pick_col, pick_row,
    dq_out, dlat_out, diq_out, diw_out, didx_out,
    qv, dov, xl, xi, sendb, recvb, kb, kt, pt, dst, sv, dpv, dqv,
    iqr, iwr, massv, mcr, mzs, mzr, dlv, wv, dsv, iqt, diqs, diws,
    gs, gown, gcr, gzs, gzr, hs, hown, hcr, hzs, hzr, ob, orx, hb, hrx, dlat_v, didx_v,
    ld_sem, iq_ss, iq_rs, iw_ss, iw_rs, xs_ss, xs_rs, ag_ss, ag_rs, dq_sem,
    m_ss, m_rs, mz_ss, mz_rs, g_ss, g_rs, gz_ss, gz_rs, h_ss, h_rs, hz_ss, hz_rs,
    o_ss, o_rs, p_ss, p_rs, b_ss, b_rs, v_ss, v_rs, fin_sem,
):
    me_k = lax.axis_index("sk")
    me_s = lax.axis_index("sq")
    z = lax.div(me_s, 2)
    c = lax.rem(me_s, 2)
    zp = lax.rem(z + 1, NZ)
    zo = lax.rem(z + 2, NZ)
    zm = lax.rem(z + 3, NZ)
    mate = z * 2 + (1 - c)

    def send(src, dst_ref, ss, rs, sk, sq):
        copy = pltpu.make_async_remote_copy(
            src_ref=src, dst_ref=dst_ref, send_sem=ss, recv_sem=rs,
            device_id=(sq, sk), device_id_type=MESH,
        )
        copy.start()
        return copy

    def arrived(dst_ref, ss, rs):
        pltpu.make_async_remote_copy(
            src_ref=dst_ref, dst_ref=dst_ref, send_sem=ss, recv_sem=rs,
            device_id=(mate, me_k), device_id_type=MESH,
        ).wait_recv()

    def peer_k(d):
        return lax.rem(me_k + d, NK)

    def from_k(d):
        return lax.rem(me_k + NK - d, NK)

    def peer_s(d):
        return lax.rem(me_s + d, NS)

    def from_s(d):
        return lax.rem(me_s + NS - d, NS)

    def rows(ref, at, count):
        return ref.at[pl.ds(pl.multiple_of(at * count, count), count)]

    sub = pl.ds(pl.multiple_of(me_s * SUB, SUB), SUB)
    loads = [
        pltpu.make_async_copy(lat_hbm.at[:, sub, :], xl, ld_sem.at[0]),
        pltpu.make_async_copy(idx_hbm.at[:, sub, :], xi, ld_sem.at[1]),
        pltpu.make_async_copy(rows(iq_hbm, me_s, QL * JL), iqr.at[me_s], ld_sem.at[2]),
        pltpu.make_async_copy(rows(iw_hbm, me_s, QL), iwr.at[me_s], ld_sem.at[3]),
        pltpu.make_async_copy(q_hbm, qv, ld_sem.at[4]),
        pltpu.make_async_copy(do_hbm, dov, ld_sem.at[5]),
    ]
    for load in loads:
        load.start()

    barrier = pltpu.get_barrier_semaphore()

    def greet_k(d, carry):
        pl.semaphore_signal(barrier, inc=1, device_id=(me_s, peer_k(d)), device_id_type=MESH)
        return carry

    def greet_s(d, carry):
        pl.semaphore_signal(barrier, inc=1, device_id=(peer_s(d), me_k), device_id_type=MESH)
        return carry

    lax.fori_loop(1, NK, greet_k, 0)
    lax.fori_loop(1, NS, greet_s, 0)
    pl.semaphore_wait(barrier, NK - 1 + NS - 1)

    loads[0].wait()
    loads[1].wait()
    pack = onehot(slot_col[...], (NK * SLOT, CH), 1)
    sendb[:, 0:KD] = dot(pack, xl[...].reshape(CH, KD)).astype(BF16)
    sendb[:, KD:IO] = jnp.zeros((NK * SLOT, IO - KD), BF16)
    sendb[:, IO:W] = dot(pack, xi[...].reshape(CH, ID)).astype(BF16)

    def ship(d, carry):
        send(rows(sendb, peer_k(d), SLOT), rows(recvb, me_k, SLOT), xs_ss.at[d], xs_rs.at[d], peer_k(d), me_s)
        return carry

    lax.fori_loop(1, NK, ship, 0)
    own = pl.ds(pl.multiple_of(me_k * SLOT, SLOT), SLOT)
    recvb[own, :] = sendb[own, :]

    def ship_iq(d, carry):
        send(rows(iq_hbm, peer_s(d), QL * JL), iqr.at[me_s], iq_ss.at[d], iq_rs.at[d], me_k, peer_s(d))
        send(rows(iw_hbm, peer_s(d), QL), iwr.at[me_s], iw_ss.at[d], iw_rs.at[d], me_k, peer_s(d))
        return carry

    lax.fori_loop(1, NS, ship_iq, 0)

    def landed(d, carry):
        arrived(rows(recvb, from_k(d), SLOT), xs_ss.at[d], xs_rs.at[d])
        return carry

    lax.fori_loop(1, NK, landed, 0)
    keep = onehot(pick_col[...], (CH, NK * SLOT), 1)
    mine = pl.ds(pl.multiple_of(me_s * CH, CH), CH)
    kb[mine, :] = dot(keep, recvb[...]).astype(BF16)

    fwd_from = jnp.where(c == 0, zm, zp)
    fwd_to = jnp.where(c == 0, zp, zm)

    def pass_on(chunk, lane, sq):
        return send(rows(kb, chunk, CH), rows(kb, chunk, CH), ag_ss.at[lane], ag_rs.at[chunk], me_k, sq)

    def chunk_here(chunk):
        arrived(rows(kb, chunk, CH), ag_ss.at[0], ag_rs.at[chunk])

    out = [
        pass_on(me_s, 0, zp * 2 + c),
        pass_on(me_s, 1, zm * 2 + c),
        pass_on(me_s, 2, mate),
    ]
    chunk_here(fwd_from * 2 + c)
    out.append(pass_on(fwd_from * 2 + c, 3, fwd_to * 2 + c))
    out.append(pass_on(fwd_from * 2 + c, 4, mate))
    chunk_here(fwd_to * 2 + c)
    out.append(pass_on(fwd_to * 2 + c, 5, mate))
    chunk_here(zo * 2 + c)
    out.append(pass_on(zo * 2 + c, 6, mate))
    for other in (z, fwd_from, fwd_to, zo):
        chunk_here(other * 2 + (1 - c))
    for copy in out:
        copy.wait_send()

    def sent_k(d, carry):
        pltpu.make_async_remote_copy(
            src_ref=rows(sendb, peer_k(d), SLOT), dst_ref=rows(recvb, me_k, SLOT),
            send_sem=xs_ss.at[d], recv_sem=xs_rs.at[d], device_id=(me_s, peer_k(d)), device_id_type=MESH,
        ).wait_send()
        return carry

    lax.fori_loop(1, NK, sent_k, 0)

    for at in range(0, KEYS, KC):
        kt[:, at:at + KC] = kb[at:at + KC, 0:IO].T
    loads[4].wait()
    loads[5].wait()
    c2 = ATTN_SCALE * LOG2E

    def attend(step, carry):
        at = pl.ds(pl.multiple_of(step * R, R), R)
        q = qv[at, :]
        do = dov[at, :]
        top = jnp.full((8, R), -jnp.inf, F32)
        for k in range(0, KEYS, KC):
            s = dot_nt(kb[k:k + KC, 0:KD], q)
            sv[k:k + KC, :] = s
            top = jnp.maximum(top, jnp.max(s.reshape(KC // 8, 8, R), axis=0))
        top = jnp.max(top, axis=0, keepdims=True) * c2
        total = jnp.zeros((8, R), F32)
        dotted = jnp.zeros((8, R), F32)
        for k in range(0, KEYS, KC):
            dp = dot_nt(kb[k:k + KC, 0:LAT], do)
            e = jnp.exp2(sv[k:k + KC, :] * c2 - top)
            sv[k:k + KC, :] = e
            dpv[k:k + KC, :] = dp
            total = total + jnp.sum(e.reshape(KC // 8, 8, R), axis=0)
            dotted = dotted + jnp.sum((e * dp).reshape(KC // 8, 8, R), axis=0)
        scale = 1.0 / jnp.sum(total, axis=0, keepdims=True)
        rowdot = jnp.sum(dotted, axis=0, keepdims=True) * scale
        for k in range(0, KEYS, KC):
            p = sv[k:k + KC, :] * scale
            pt[k:k + KC, at] = p.astype(BF16)
            dst[k:k + KC, at] = (p * (dpv[k:k + KC, :] - rowdot)).astype(BF16)
        dq = dot(kt[...], dst[:, at]) * ATTN_SCALE
        dqv[at, :] = dq.T[:, 0:KD].astype(BF16)
        pltpu.make_async_copy(dqv.at[at], dq_out.at[at], dq_sem.at[step]).start()
        return carry

    lax.fori_loop(0, ROWS // R, attend, 0)

    same_query = lax.div(lax.broadcasted_iota(jnp.int32, (QT, ROWS), 1), HL) == lax.broadcasted_iota(
        jnp.int32, (QT, ROWS), 0
    )
    pool = jnp.where(same_query, 1.0, 0.0).astype(BF16)
    for k in range(0, KEYS, KC):
        massv[:, k:k + KC] = dot_nt(pool, pt[k:k + KC, :])

    def mass_pair(i, carry):
        send(rows(massv, 2 * i + (1 - c), QL), mcr.at[i], m_ss.at[i], m_rs.at[i], me_k, mate)
        return carry

    lax.fori_loop(0, NZ, mass_pair, 0)

    def mass_sum(d):
        there = lax.rem(z + d, NZ)
        arrived(mcr.at[there], m_ss.at[there], m_rs.at[there])
        return massv[pl.ds(pl.multiple_of((2 * there + c) * QL, QL), QL), :] + mcr[there]

    for d in (2, 1, 3):
        mzs[d] = mass_sum(d)
        send(mzs.at[d], mzr.at[d], mz_ss.at[d], mz_rs.at[d], me_k, lax.rem(z + d, NZ) * 2 + c)
    mzs[0] = mass_sum(0)

    def key_grad(chunk):
        at = pl.ds(pl.multiple_of(chunk * CH, CH), CH)
        both = dot(dst[at, :], qv[...]) * ATTN_SCALE
        value = dot(pt[at, :], dov[...])
        return both[:, 0:LAT] + value, both[:, LAT:KD]

    def pair_chunk(i, carry):
        there = lax.rem(z + 2 + i, NZ)
        main, rope = key_grad(2 * there + (1 - c))
        gs[there, :, 0:LAT] = main.astype(BF16)
        gs[there, :, LAT:KD] = rope.astype(BF16)
        send(gs.at[there], gcr.at[there], g_ss.at[there], g_rs.at[there], me_k, mate)
        return carry

    lax.fori_loop(0, NZ, pair_chunk, 0)

    def own_chunk(i, carry):
        there = lax.rem(z + 2 + i, NZ)
        main, rope = key_grad(2 * there + c)
        arrived(gcr.at[there], g_ss.at[there], g_rs.at[there])
        gown[:, 0:LAT] = main + gcr[there, :, 0:LAT].astype(F32)
        gown[:, LAT:KD] = rope + gcr[there, :, LAT:KD].astype(F32)

        @pl.when(i != 2)
        def _():
            gzs[there] = gown[...].astype(BF16)
            send(gzs.at[there], gzr.at[z], gz_ss.at[there], gz_rs.at[z], me_k, there * 2 + c)

        @pl.when(i == 2)
        def _():
            hown[...] = gown[...]

        return carry

    lax.fori_loop(0, NZ, own_chunk, 0)

    loads[2].wait()
    loads[3].wait()

    def iq_here(d, carry):
        arrived(iqr.at[from_s(d)], iq_ss.at[d], iq_rs.at[d])
        arrived(iwr.at[from_s(d)], iw_ss.at[d], iw_rs.at[d])
        return carry

    lax.fori_loop(1, NS, iq_here, 0)
    eye = lax.broadcasted_iota(jnp.int32, (JL, 128), 0) == lax.broadcasted_iota(jnp.int32, (JL, 128), 1)
    eye8 = lax.broadcasted_iota(jnp.int32, (JL, JL), 0) == lax.broadcasted_iota(jnp.int32, (JL, JL), 1)

    dlv[...] = jnp.zeros_like(dlv)

    def logit_part(src, carry):
        weight = jnp.where(eye8[None], iwr[src][:, None, :], 0.0)
        weight = jnp.sum(weight, axis=2, keepdims=True).reshape(QL * JL, 1)
        wv[src] = jnp.broadcast_to(weight, (QL * JL, 128))
        sim = dot_nt(iqr[src], kb[:, IO:W])
        dlv[...] += jnp.maximum(sim, 0.0) * weight
        iqt[:, pl.ds(pl.multiple_of(src * 128, 128), 128)] = iqr[src].T
        return carry

    lax.fori_loop(0, NS, logit_part, 0)
    logits = INDEX_SCALE * jnp.sum(dlv[...].reshape(QL, JL, KEYS), axis=1)
    e = jnp.exp(logits - jnp.max(logits, axis=1, keepdims=True))
    guess = e / jnp.sum(e, axis=1, keepdims=True)
    mass = mzs[0]
    for d in (1, 2, 3):
        arrived(mzr.at[d], mz_ss.at[d], mz_rs.at[d])
        mass = mass + mzr[d]
    dlogit = INDEX_SCALE * (guess - mass * (1.0 / H))
    dlv[...] = jnp.broadcast_to(dlogit[:, None, :], (QL, JL, KEYS)).reshape(QL * JL, KEYS)

    def index_part(src, carry):
        sim = dot_nt(iqr[src], kb[:, IO:W])
        dl = dlv[...]
        ds = jnp.where(sim > 0, dl * wv[src][:, 0:1], 0.0).astype(BF16)
        dsv[pl.ds(pl.multiple_of(src * 128, 128), 128), :] = ds
        dw = jnp.sum(dl * jnp.maximum(sim, 0.0), axis=1, keepdims=True).reshape(QL, JL, 1)
        diws[src] = jnp.sum(jnp.where(eye[None], dw, 0.0), axis=1)[:, 0:JL]
        diqs[src] = dot(ds, kb[:, IO:W])
        return carry

    lax.fori_loop(0, NS, index_part, 0)

    def ship_grads(d, carry):
        there = peer_s(d)
        send(diqs.at[there], rows(diq_out, me_s, QL * JL), b_ss.at[d], b_rs.at[d], me_k, there)
        send(diws.at[there], rows(diw_out, me_s, QL), v_ss.at[d], v_rs.at[d], me_k, there)
        return carry

    lax.fori_loop(1, NS, ship_grads, 0)
    here_iq = pltpu.make_async_copy(diqs.at[me_s], rows(diq_out, me_s, QL * JL), fin_sem.at[0])
    here_iw = pltpu.make_async_copy(diws.at[me_s], rows(diw_out, me_s, QL), fin_sem.at[1])
    here_iq.start()
    here_iw.start()

    expand = onehot(pick_row[...], (NK * SLOT, CH), 0)
    home = onehot(slot_row[...], (CH, NK * SLOT), 0)

    def ship_home(buf, got, ss, rs):
        def one(d, carry):
            send(rows(buf, peer_k(d), SLOT), rows(got, me_k, SLOT), ss.at[d], rs.at[d], peer_k(d), me_s)
            return carry

        lax.fori_loop(1, NK, one, 0)
        got[own, :] = buf[own, :]

    def all_home(got, ss, rs):
        def one(d, carry):
            arrived(rows(got, from_k(d), SLOT), ss.at[d], rs.at[d])
            return carry

        lax.fori_loop(1, NK, one, 0)

    def all_sent(buf, got, ss, rs):
        def one(d, carry):
            pltpu.make_async_remote_copy(
                src_ref=rows(buf, peer_k(d), SLOT), dst_ref=rows(got, me_k, SLOT),
                send_sem=ss.at[d], recv_sem=rs.at[d], device_id=(me_s, peer_k(d)), device_id_type=MESH,
            ).wait_send()
            return carry

        lax.fori_loop(1, NK, one, 0)

    acc = hown[...]
    for other in (zp, zm, zo):
        arrived(gzr.at[other], gz_ss.at[other], gz_rs.at[other])
        acc = acc + gzr[other].astype(F32)
    ob[...] = dot(expand, acc.astype(BF16)).astype(BF16)
    ship_home(ob, orx, o_ss, o_rs)

    for k in range(0, KEYS, KC):
        part = dot(iqt[...], dsv[:, k:k + KC])
        sv[k:k + KC, 0:ID] = part.T

    def pair_index(i, carry):
        there = lax.rem(z + 2 + i, NZ)
        at = pl.ds(pl.multiple_of((2 * there + (1 - c)) * CH, CH), CH)
        hs[there] = sv[at, 0:ID].astype(BF16)
        send(hs.at[there], hcr.at[there], h_ss.at[there], h_rs.at[there], me_k, mate)
        return carry

    lax.fori_loop(0, NZ, pair_index, 0)

    def index_sum(there):
        at = pl.ds(pl.multiple_of((2 * there + c) * CH, CH), CH)
        arrived(hcr.at[there], h_ss.at[there], h_rs.at[there])
        return sv[at, 0:ID] + hcr[there].astype(F32)

    for there in (zo, zp, zm):
        hzs[there] = index_sum(there).astype(BF16)
        send(hzs.at[there], hzr.at[z], hz_ss.at[there], hz_rs.at[z], me_k, there * 2 + c)
    acc = index_sum(z)
    for other in (zp, zm, zo):
        arrived(hzr.at[other], hz_ss.at[other], hz_rs.at[other])
        acc = acc + hzr[other].astype(F32)
    hb[...] = dot(expand, acc.astype(BF16)).astype(BF16)
    ship_home(hb, hrx, p_ss, p_rs)

    all_home(orx, o_ss, o_rs)
    dlat_v[...] = dot(home, orx[...]).reshape(NK, SUB, KD)
    out_lat = pltpu.make_async_copy(dlat_v, dlat_out, fin_sem.at[2])
    out_lat.start()
    all_home(hrx, p_ss, p_rs)
    didx_v[...] = dot(home, hrx[...]).reshape(NK, SUB, ID)
    out_idx = pltpu.make_async_copy(didx_v, didx_out, fin_sem.at[3])
    out_idx.start()

    def grads_here(d, carry):
        arrived(rows(diq_out, from_s(d), QL * JL), b_ss.at[d], b_rs.at[d])
        arrived(rows(diw_out, from_s(d), QL), v_ss.at[d], v_rs.at[d])
        return carry

    lax.fori_loop(1, NS, grads_here, 0)

    def sent_s(d, carry):
        def gone(src, dst_ref, ss, rs):
            pltpu.make_async_remote_copy(
                src_ref=src, dst_ref=dst_ref, send_sem=ss.at[d], recv_sem=rs.at[d],
                device_id=(peer_s(d), me_k), device_id_type=MESH,
            ).wait_send()

        gone(rows(iq_hbm, peer_s(d), QL * JL), iqr.at[me_s], iq_ss, iq_rs)
        gone(rows(iw_hbm, peer_s(d), QL), iwr.at[me_s], iw_ss, iw_rs)
        gone(diqs.at[peer_s(d)], rows(diq_out, me_s, QL * JL), b_ss, b_rs)
        gone(diws.at[peer_s(d)], rows(diw_out, me_s, QL), v_ss, v_rs)
        return carry

    lax.fori_loop(1, NS, sent_s, 0)

    def gone(src, dst_ref, ss, rs):
        pltpu.make_async_remote_copy(
            src_ref=src, dst_ref=dst_ref, send_sem=ss, recv_sem=rs,
            device_id=(mate, me_k), device_id_type=MESH,
        ).wait_send()

    def sent_z(i, carry):
        gone(rows(massv, 2 * i + (1 - c), QL), mcr.at[i], m_ss.at[i], m_rs.at[i])
        gone(gs.at[i], gcr.at[i], g_ss.at[i], g_rs.at[i])
        gone(hs.at[i], hcr.at[i], h_ss.at[i], h_rs.at[i])
        return carry

    lax.fori_loop(0, NZ, sent_z, 0)
    for d in (1, 2, 3):
        there = lax.rem(z + d, NZ)
        gone(mzs.at[d], mzr.at[d], mz_ss.at[d], mz_rs.at[d])
        gone(gzs.at[there], gzr.at[z], gz_ss.at[there], gz_rs.at[z])
        gone(hzs.at[there], hzr.at[z], hz_ss.at[there], hz_rs.at[z])
    all_sent(ob, orx, o_ss, o_rs)
    all_sent(hb, hrx, p_ss, p_rs)

    def dq_done(step, carry):
        at = pl.ds(pl.multiple_of(step * R, R), R)
        pltpu.make_async_copy(dqv.at[at], dq_out.at[at], dq_sem.at[step]).wait()
        return carry

    lax.fori_loop(0, ROWS // R, dq_done, 0)
    here_iq.wait()
    here_iw.wait()
    out_lat.wait()
    out_idx.wait()


def body(queries, out_grad, latent_keys, index_queries, index_weights, index_keys, picks):
    my_column = lax.axis_index("sk")
    owner = picks // NK
    local = picks % NK
    place = jnp.arange(PICKS, dtype=jnp.int32)
    rank = jnp.sum((owner[:, :, None] == owner[:, None, :]) & (place[None, :] < place[:, None])[None], axis=2)
    slot = owner * CAP + rank
    mine = lax.dynamic_index_in_dim(slot, my_column, 0, keepdims=False)
    row = jnp.arange(SUB, dtype=jnp.int32)
    pick_at = (mine[:, None] * SUB + row).reshape(-1)
    hit = slot[:, None, :] == (my_column * CAP + jnp.arange(CAP, dtype=jnp.int32))[None, :, None]
    block = jnp.sum(jnp.where(hit, local[:, None, :] + 1, 0), axis=2) - 1
    slot_at = jnp.where(block[:, :, None] >= 0, block[:, :, None] * SUB + row, -1).reshape(-1)

    hbm = pl.BlockSpec(memory_space=pl.ANY)
    vmem = pl.BlockSpec(memory_space=pltpu.VMEM)
    dma = pltpu.SemaphoreType.DMA
    v = pltpu.VMEM
    outs = pl.pallas_call(
        kernel,
        out_shape=[
            jax.ShapeDtypeStruct((ROWS, KD), BF16),
            jax.ShapeDtypeStruct((NK, SUB, KD), F32),
            jax.ShapeDtypeStruct((QT * JL, ID), F32),
            jax.ShapeDtypeStruct((QT, JL), F32),
            jax.ShapeDtypeStruct((NK, SUB, ID), F32),
        ],
        in_specs=[hbm] * 6 + [vmem] * 4,
        out_specs=[hbm] * 5,
        scratch_shapes=[
            v((ROWS, KD), BF16), v((ROWS, LAT), BF16),
            v((NK, SUB, KD), BF16), v((NK, SUB, ID), BF16),
            v((NK * SLOT, W), BF16), v((NK * SLOT, W), BF16), v((KEYS, W), BF16),
            v((IO, KEYS), BF16), v((KEYS, ROWS), BF16), v((KEYS, ROWS), BF16),
            v((KEYS, R), F32), v((KEYS, R), F32), v((ROWS, KD), BF16),
            v((NS, QL * JL, ID), BF16), v((NS, QL, JL), F32),
            v((QT, KEYS), F32), v((NZ, QL, KEYS), F32), v((NZ, QL, KEYS), F32), v((NZ, QL, KEYS), F32),
            v((QL * JL, KEYS), F32), v((NS, QL * JL, 128), F32),
            v((NS * QL * JL, KEYS), BF16), v((ID, NS * QL * JL), BF16),
            v((NS, QL * JL, ID), F32), v((NS, QL, JL), F32),
            v((NZ, CH, KD), BF16), v((CH, KD), F32), v((NZ, CH, KD), BF16),
            v((NZ, CH, KD), BF16), v((NZ, CH, KD), BF16),
            v((NZ, CH, ID), BF16), v((CH, KD), F32), v((NZ, CH, ID), BF16),
            v((NZ, CH, ID), BF16), v((NZ, CH, ID), BF16),
            v((NK * SLOT, KD), BF16), v((NK * SLOT, KD), BF16),
            v((NK * SLOT, ID), BF16), v((NK * SLOT, ID), BF16),
            v((NK, SUB, KD), F32), v((NK, SUB, ID), F32),
            dma((6,)), dma((NS,)), dma((NS,)), dma((NS,)), dma((NS,)),
            dma((NK,)), dma((NK,)), dma((NS,)), dma((NS,)), dma((NS,)),
            dma((NZ,)), dma((NZ,)), dma((NZ,)), dma((NZ,)),
            dma((NZ,)), dma((NZ,)), dma((NZ,)), dma((NZ,)),
            dma((NZ,)), dma((NZ,)), dma((NZ,)), dma((NZ,)),
            dma((NK,)), dma((NK,)), dma((NK,)), dma((NK,)),
            dma((NS,)), dma((NS,)), dma((NS,)), dma((NS,)), dma((4,)),
        ],
        compiler_params=pltpu.CompilerParams(
            collective_id=0, has_side_effects=True, vmem_limit_bytes=63 * 1024 * 1024
        ),
        name="sparse_attention_backward",
    )(
        queries.reshape(ROWS, KD),
        out_grad.reshape(ROWS, LAT),
        latent_keys,
        index_queries.reshape(QT * JL, ID),
        index_weights,
        index_keys,
        slot_at[:, None],
        slot_at[None, :],
        pick_at[:, None],
        pick_at[None, :],
    )
    dq, dlat, diq, diw, didx = outs
    return (dq.reshape(QT, HL, KD), dlat, diq.reshape(QT, JL, ID), diw, didx)


def solution(mesh):
    placed = (
        P("sk", "sq", None),
        P("sk", "sq", None),
        P("sk", None, None),
        P("sk", "sq", None),
        P("sk", "sq"),
        P("sk", None, None),
        P(),
    )
    return jax.shard_map(
        body,
        mesh=mesh,
        in_specs=placed,
        out_specs=(
            P("sk", "sq", None),
            P("sk", "sq", None),
            P("sk", "sq", None),
            P("sk", "sq"),
            P("sk", "sq", None),
        ),
        check_vma=False,
    )
```

time: 543 us -> 137 us (0.25)
  waiting for transfers between devices: 262 us -> 0 us
  Pallas kernels: 0 us -> 114 us
  matrix products: 85.3 us -> 0 us
  local copies, waits for them, and re-layouts: 95.7 us -> 19.9 us
  other arithmetic: 55.5 us -> 2.23 us
  starting transfers between devices: 26.4 us -> 0 us
  between operations: 14.4 us -> 0.73 us
    all_to_all x4 -> x0, waiting for transfers between devices: 188 us -> none  [the longest x1 129 us: body(): lax.all_to_all(latent_slots, 'sk', split_axis=0, concat_axis=0, tiled=True)]
    pallas_call x0 -> x1, Pallas kernels: none -> 114 us  [body(): pl.pallas_call(kernel, out_shape=[jax.ShapeDtypeStruct((ROWS, KD), BF16),...]
    dot_general x10 -> x0, matrix products: 85.3 us -> none  [the longest x1 19.1 us: body(): jnp.einsum('qhk,qhv->kv', attn_probs.astype(jnp.bfloat16), out_grad, pref...]
    psum x1 -> x0, waiting for transfers between devices: 51 us -> none  [body(): logits, mass_total = lax.psum((partial_logit, head_mass), 'sq')]
    reshape x4 -> x0, local copies, waits for them, and re-layouts: 36.3 us -> none  [the longest x1 17.1 us: body(): latent_slots = jnp.zeros((slot_total, block_rows, key_width), jnp.float32...]
    all_to_all x4 -> x0, starting transfers between devices: 25.9 us -> none  [the longest x1 7.33 us: body(): lax.all_to_all(latent_slots, 'sk', split_axis=0, concat_axis=0, tiled=True)]
    reduce_scatter x2 -> x0, waiting for transfers between devices: 22.7 us -> none  [the longest x1 22.7 us: body(): lax.psum_scatter(densify(onehot, got_latent), 'sq', scatter_dimension=1,...]
    sub x1 -> x0, other arithmetic: 17.9 us -> none  [body(): attn_probs = jax.nn.softmax(scores, axis=-1)]
  transfers between devices with their start and end apart: 7 -> 0, of which waited for: 5 -> 0; matrix products, arithmetic and copies ran while one was open for 29% -> 0% of each run, Pallas kernels for 0% -> 0%
where the time goes in v1:
time: 137 us
  Pallas kernels  114 us (83%)
  local copies, waits for them, and re-layouts  19.9 us (15%)
  other arithmetic  2.23 us (2%)
    pallas_call x1, Pallas kernels, body(): pl.pallas_call(kernel, out_shape=[jax.ShapeDtypeStruct((ROWS, KD), BF16),...  114 us
    unnamed x18, local copies, waits for them, and re-layouts  16.8 us

profile of v1, /device:TPU:0, one launch (start us, length us, event | category | flops | bytes accessed | tf_op | source)
XLA Modules:
  0.0 136.9 jit_solution(14458122071934526009)
XLA Ops:
  0.7 0.7 add_select_fusion.2
  1.4 0.4 convert_reduce_fusion
  1.8 0.7 multiply_add_fusion
  2.5 0.2 select_reduce_fusion
  2.7 0.1 copy.25
  2.8 0.1 copy.26
  2.9 0.1 add_select_fusion
  3.0 0.7 select_n.49.slot_row
  3.7 0.1 iota_add_fusion
  3.8 0.6 add.109.pick_row
  4.4 1.4 %copy.28.iw_hbm = f32[128,8]{1,0:T(8,128)} copy(f32[128,8]{0,1:T(8,128)} %param.11) | data formatting | bytes 8192 | tf_op args[4]
  5.8 0.8 add.110.pick_col
  6.6 0.9 select_n.51.slot_col
  7.5 0.0 copy-start
  7.5 5.1 %copy.24 = bf16[128,16,576]{2,1,0:T(8,128)(2,1)} copy(bf16[128,16,576]{0,2,1:T(8,128)(2,1)} %param.7) | data formatting | bytes 4718592 | tf_op args[0]
  12.5 0.0 copy-done
  12.5 2.6 %copy.27.lat_hbm = bf16[16,128,576]{2,1,0:T(8,128)(2,1)} copy(bf16[16,128,576]{1,2,0:T(8,128)(2,1)S(1)} %copy-done) | data formatting | bytes 4718592 | tf_op args[2]
  15.1 114.1 %sparse_attention_backward.1 = (bf16[2048,576]{1,0:T(8,128)(2,1)}, f32[16,16,576]{2,1,0:T(8,128)}, f32[1024,128]{1,0:T(8,128)}, f32[128,8]{1,0:T(8,128)}, f32[16,16,128]{2,1,0:T(8,128)}) custom-call(bf16[2048,576]{1,0:T(8,128)(2,1)} %bitcast.7, bf16[2048,512]{1,0:T(8,128)(2,1)} %bitcast.9, bf16[16,128,576]{2,1,0:T(8,128)(2,1)} %copy.27.lat_hbm, ...), custom_call_target="tpu_custom_call" | custom-call | tf_op jit(solution)/shard_map/sparse_attention_backward/pallas_call | solution.py:496
  129.2 0.0 copy-start.4
  129.2 0.0 copy-start.1
  129.2 0.0 copy-start.2
  129.2 4.8 %copy.31 = bf16[128,16,576]{0,2,1:T(8,128)(2,1)} copy(bf16[128,16,576]{2,1,0:T(8,128)(2,1)} %bitcast.8) | data formatting | bytes 4718592
  134.0 0.0 copy-done.4
  134.0 0.0 copy-start.3
  134.0 0.7 copy.32
  134.6 0.0 copy-done.1
  134.6 0.8 copy.36
  135.5 0.0 copy-done.2
  135.5 0.8 copy.37
  136.3 0.0 copy-done.3
  136.3 0.7 copy.38
  (5 shorter events, 0.0 us)
Async XLA Ops:
  7.5 5.1 %copy-start = (bf16[16,128,576]{1,2,0:T(8,128)(2,1)S(1)}, bf16[16,128,576]{1,2,0:T(8,128)(2,1)}, u32[]{:S(2)}) copy-start(bf16[16,128,576]{1,2,0:T(8,128)(2,1)} %param.9) | copy-start | bytes 7077892
  129.2 4.8 %copy-start.4 = (f32[128,8]{1,0:T(8,128)S(1)}, f32[128,8]{1,0:T(8,128)}, u32[]{:S(2)}) copy-start(f32[128,8]{1,0:T(8,128)} %get-tuple-element.28) | copy-start | bytes 12292
  129.2 5.5 %copy-start.1 = (f32[16,16,576]{2,1,0:T(8,128)S(1)}, f32[16,16,576]{2,1,0:T(8,128)}, u32[]{:S(2)}) copy-start(f32[16,16,576]{2,1,0:T(8,128)} %get-tuple-element.38) | copy-start | bytes 1769476
  129.2 6.3 %copy-start.2 = (f32[1024,128]{1,0:T(8,128)S(1)}, f32[1024,128]{1,0:T(8,128)}, u32[]{:S(2)}) copy-start(f32[1024,128]{1,0:T(8,128)} %get-tuple-element.12) | copy-start | bytes 1572868
  134.0 2.3 %copy-start.3 = (f32[16,16,128]{2,1,0:T(8,128)S(1)}, f32[16,16,128]{2,1,0:T(8,128)}, u32[]{:S(2)}) copy-start(f32[16,16,128]{2,1,0:T(8,128)} %get-tuple-element.41) | copy-start | bytes 393220

commit v2 on v0

v2 whole, which is shorter than its diff:
```python
import math

import jax
import jax.numpy as jnp
from jax import lax
from jax.experimental import pallas as pl
from jax.experimental.pallas import tpu as pltpu
from jax.sharding import PartitionSpec as P

H = 128
HI = 64
ID = 128
CAP = 2
LAT = 512
KD = 576
ATTN_SCALE = 0.1353
INDEX_SCALE = 1.0 / math.sqrt(ID * HI)
LOG2E = 1.4426950408889634

MESH = pl.DeviceIdType.MESH
F32 = jnp.float32
BF16 = jnp.bfloat16

NK = 16
NS = 8
NZ = 4
SUB = 16
PICKS = 16
CH = PICKS * SUB
KEYS = NS * CH
QT = 128
HL = 16
ROWS = HL * QT
JL = 8
QL = 16
QJ = QL * JL
SLOTS = NK * CAP
W = 768
IO = 640
GW = 256
GROUPS = 3
R = 256
KC = 256


def dot(a, b):
    return jnp.dot(a, b, preferred_element_type=F32)


def dot_nt(a, b):
    return lax.dot_general(a, b, (((1,), (1,)), ((), ())), preferred_element_type=F32)


def dot_tn(a, b):
    return lax.dot_general(a, b, (((0,), (0,)), ((), ())), preferred_element_type=F32)


def iota(shape, axis):
    return lax.broadcasted_iota(jnp.int32, shape, axis)


def ones_where(hit):
    return jnp.where(hit, 1.0, 0.0).astype(BF16)


def kernel(
    q_hbm, do_hbm, lat_hbm, iq_hbm, iw_hbm, idx_hbm, picks,
    dq_out, dlat_out, diq_out, diw_out, didx_out,
    qt, dov, xi, xs, sendb, recvb, kb, to_slot, to_block, sv, pt, dst, dqv, topv, totv, dotv,
    iqr, iwr, wv, lgv, masst, mcr, mzs, mzr, iqt, diws, diwr,
    gs, gcr, gzs, gzr, ob, orx, dlat_v, didx_v, diw_v, found,
    ld_sem, q_sem, lat_sem, iq_ss, iq_rs, iw_ss, iw_rs, xs_ss, xs_rs, ag_ss, ag_rs, dq_sem,
    m_ss, m_rs, mz_ss, mz_rs, g_ss, g_rs, gz_ss, gz_rs, o_ss, o_rs, b_ss, b_rs, v_ss, v_rs, fin_sem,
):
    massq = sv.at[0:QT]
    dlv = sv.at[QT:QT + QJ]
    ikt = sv.at[256:256 + ID]
    gown = sv.at[512:512 + GROUPS * 512, 0:NZ * GW]
    diqs = sv.at[512:512 + NS * QJ, NZ * GW:NZ * GW + ID]

    me_k = lax.axis_index("sk")
    me_s = lax.axis_index("sq")
    z = lax.div(me_s, 2)
    c = lax.rem(me_s, 2)
    zp = lax.rem(z + 1, NZ)
    zo = lax.rem(z + 2, NZ)
    zm = lax.rem(z + 3, NZ)
    mate = z * 2 + (1 - c)

    def remote(src, dst_ref, ss, rs, sk, sq):
        return pltpu.make_async_remote_copy(
            src_ref=src, dst_ref=dst_ref, send_sem=ss, recv_sem=rs,
            device_id=(sq, sk), device_id_type=MESH,
        )

    def send(*what):
        remote(*what).start()

    def gone(src, dst_ref, ss, rs):
        remote(src, dst_ref, ss, rs, me_k, mate).wait_send()

    def arrived(dst_ref, ss, rs):
        remote(dst_ref, dst_ref, ss, rs, me_k, mate).wait_recv()

    def peer_k(d):
        return lax.rem(me_k + d, NK)

    def from_k(d):
        return lax.rem(me_k + NK - d, NK)

    def peer_s(d):
        return lax.rem(me_s + d, NS)

    def from_s(d):
        return lax.rem(me_s + NS - d, NS)

    def span(at, count):
        return pl.ds(pl.multiple_of(at * count, count), count)

    def rows(ref, at, count):
        return ref.at[span(at, count)]

    def loop(lo, hi, step):
        def one(i, carry):
            step(i)
            return carry

        lax.fori_loop(lo, hi, one, 0)

    load_idx = pltpu.make_async_copy(idx_hbm.at[:, span(me_s, SUB), :], xi, ld_sem.at[0])
    load_iq = pltpu.make_async_copy(rows(iq_hbm, me_s, QJ), iqr.at[me_s], ld_sem.at[1])
    load_iw = pltpu.make_async_copy(iw_hbm, iwr.at[me_s], ld_sem.at[2])
    load_do = pltpu.make_async_copy(do_hbm, pt.at[:, 0:LAT], ld_sem.at[3])
    load_lat = [
        pltpu.make_async_copy(lat_hbm.at[b], dst.at[0:KD, b * 128:(b + 1) * 128], lat_sem.at[b]) for b in range(NK)
    ]
    load_q = [pltpu.make_async_copy(q_hbm.at[h], qt.at[:, h * QT:(h + 1) * QT], q_sem.at[h]) for h in range(HL)]
    for load in load_lat + [load_idx]:
        load.start()

    barrier = pltpu.get_barrier_semaphore()

    def greet_k(d):
        pl.semaphore_signal(barrier, inc=1, device_id=(me_s, peer_k(d)), device_id_type=MESH)

    def greet_s(d):
        pl.semaphore_signal(barrier, inc=1, device_id=(peer_s(d), me_k), device_id_type=MESH)

    loop(1, NK, greet_k)
    loop(1, NS, greet_s)

    def picked(t):
        first = jnp.int32(-1)
        second = jnp.int32(-1)
        for p in range(PICKS):
            block = picks[t, p]
            local = block & (NK - 1)
            here = lax.shift_right_logical(block, 4) == me_k
            second = jnp.where(here & (first >= 0), local, second)
            first = jnp.where(here & (first < 0), local, first)
        found[t, 0] = first
        found[t, 1] = second

    loop(0, NK, picked)

    pick_rows = ones_where(iota((SUB, 128), 1) == me_s * SUB + iota((SUB, 128), 0))
    load_idx.wait()
    for b in range(NK):
        load_lat[b].wait()
        xs[b, :, 0:KD] = dot_nt(pick_rows, dst[0:KD, b * 128:(b + 1) * 128]).astype(BF16)
        xs[b, :, KD:IO] = jnp.zeros((SUB, IO - KD), BF16)
        xs[b, :, IO:W] = xi[b]
    cell = iota((SUB, CH), 1) - iota((SUB, CH), 0)

    for load in [load_do] + load_q + [load_iq, load_iw]:
        load.start()

    def pack(t):
        sendb[2 * t] = xs[jnp.maximum(found[t, 0], 0)]
        sendb[2 * t + 1] = xs[jnp.maximum(found[t, 1], 0)]

    loop(0, NK, pack)
    pl.semaphore_wait(barrier, NK - 1 + NS - 1)

    def slots(ref, k):
        return ref.at[pl.ds(2 * k, 2)]

    loop(1, NK, lambda d: send(
        slots(sendb, peer_k(d)), slots(recvb, me_k), xs_ss.at[d], xs_rs.at[d], peer_k(d), me_s))
    recvb[pl.ds(2 * me_k, 2)] = sendb[pl.ds(2 * me_k, 2)]

    def ship_iq(d):
        send(rows(iq_hbm, peer_s(d), QJ), iqr.at[me_s], iq_ss.at[d], iq_rs.at[d], me_k, peer_s(d))
        send(iw_hbm, iwr.at[me_s], iw_ss.at[d], iw_rs.at[d], me_k, peer_s(d))

    loop(1, NS, ship_iq)

    def place(t):
        to_block[span(2 * t, SUB), :] = ones_where(cell == found[t, 0] * SUB)
        to_block[span(2 * t + 1, SUB), :] = ones_where(cell == found[t, 1] * SUB)

    mine = [picks[me_k, p] for p in range(PICKS)]
    owner = [lax.shift_right_logical(block, 4) for block in mine]
    slot = []
    for p in range(PICKS):
        rank = jnp.int32(0)
        for before in range(p):
            rank = rank + jnp.where(owner[before] == owner[p], 1, 0)
        slot.append(owner[p] * CAP + rank)

    def unpick(s):
        pick = jnp.int32(-1)
        for p in range(PICKS):
            pick = jnp.where(slot[p] == s, p, pick)
        to_slot[span(s, SUB), :] = ones_where(cell == pick * SUB)

    loop(0, SLOTS, unpick)
    loop(0, NK, place)
    i0, i1 = iota((CH, CH), 0), iota((CH, CH), 1)
    swap = ones_where(i1 == lax.rem(i0, 16) * 16 + lax.div(i0, 16))
    load_do.wait()
    for g in range(QT // 16):
        turned = dot(swap, pt[g * CH:(g + 1) * CH, 0:LAT]).astype(BF16)
        for h in range(HL):
            dov[h * QT + g * 16:h * QT + (g + 1) * 16, :] = turned[h * 16:(h + 1) * 16]
    for load in load_q:
        load.wait()
    topv[...] = jnp.full(topv.shape, -jnp.inf, F32)
    totv[...] = jnp.zeros_like(totv)
    dotv[...] = jnp.zeros_like(dotv)
    masst[...] = jnp.zeros_like(masst)

    load_iq.wait()
    load_iw.wait()

    def iq_here(d):
        arrived(iqr.at[from_s(d)], iq_ss.at[d], iq_rs.at[d])
        arrived(iwr.at[from_s(d)], iw_ss.at[d], iw_rs.at[d])

    loop(1, NS, iq_here)
    my_query = iota((QL, JL, 128), 2) == me_s * QL + iota((QL, JL, 128), 0)

    def weigh(src):
        weight = jnp.where(my_query, iwr[src][None], 0.0)
        weight = jnp.sum(weight, axis=2, keepdims=True).reshape(QJ, 1)
        wv[src] = jnp.broadcast_to(weight, (QJ, 128))
        iqt[:, span(src, 128)] = iqr[src].T

    loop(0, NS, weigh)

    fwd_from = jnp.where(c == 0, zm, zp)
    fwd_to = jnp.where(c == 0, zp, zm)
    lanes = {}
    c2 = ATTN_SCALE * LOG2E

    def pass_on(chunk, lane, sq):
        lanes[lane] = chunk
        send(rows(kb, chunk, CH), rows(kb, chunk, CH), ag_ss.at[lane], ag_rs.at[chunk], me_k, sq)

    def chunk_here(chunk):
        arrived(rows(kb, chunk, CH), ag_ss.at[0], ag_rs.at[chunk])

    def meet(chunk):
        at = span(chunk, CH)

        for lo in range(0, ROWS, 512):
            lane = slice(lo, lo + 512)
            s = dot(kb[at, 0:KD], qt[:, lane]) * c2
            dp = dot_nt(kb[at, 0:LAT], dov[lane, :])
            sv[at, lane] = s
            s = s.reshape(CH // 8, 8, 512)
            old = topv[:, lane]
            top = jnp.maximum(old, jnp.max(s, axis=0))
            e = jnp.exp2(s - top[None])
            fade = jnp.exp2(old - top)
            topv[:, lane] = top
            totv[:, lane] = totv[:, lane] * fade + jnp.sum(e, axis=0)
            dotv[:, lane] = dotv[:, lane] * fade + jnp.sum(e * dp.reshape(CH // 8, 8, 512), axis=0)

        keys = kb[at, IO:W]
        acc = jnp.zeros((QJ, CH), F32)
        for src in range(NS):
            acc = acc + jnp.maximum(dot_nt(iqr[src], keys), 0.0) * jnp.tile(wv[src], (1, CH // 128))
        lgv[:, at] = INDEX_SCALE * jnp.sum(acc.reshape(QL, JL, CH), axis=1)

    def meet_mate(zz):
        chunk_here(zz * 2 + (1 - c))
        meet(zz * 2 + (1 - c))

    loop(1, NK, lambda d: arrived(slots(recvb, from_k(d)), xs_ss.at[d], xs_rs.at[d]))
    for p in range(PICKS):
        kb[pl.ds(pl.multiple_of(me_s * CH + p * SUB, SUB), SUB), :] = recvb[slot[p]]
    pass_on(me_s, 0, mate)
    pass_on(me_s, 1, fwd_to * 2 + c)
    meet(me_s)
    pass_on(me_s, 2, fwd_from * 2 + c)
    chunk_here(fwd_from * 2 + c)
    pass_on(fwd_from * 2 + c, 3, fwd_to * 2 + c)
    pass_on(fwd_from * 2 + c, 4, mate)
    meet_mate(z)
    meet(fwd_from * 2 + c)
    chunk_here(fwd_to * 2 + c)
    pass_on(fwd_to * 2 + c, 5, mate)
    meet_mate(fwd_to)
    meet(fwd_to * 2 + c)
    chunk_here(zo * 2 + c)
    pass_on(zo * 2 + c, 6, mate)
    meet_mate(fwd_from)
    meet(zo * 2 + c)
    meet_mate(zo)

    def attend(step):
        at = span(step, R)
        do = dov[at, :]
        top = jnp.max(topv[:, at], axis=0, keepdims=True)
        fade = jnp.exp2(topv[:, at] - top)
        total = jnp.sum(totv[:, at] * fade, axis=0, keepdims=True)
        rowdot = jnp.sum(dotv[:, at] * fade, axis=0, keepdims=True) / total
        top = top + jnp.log2(total)
        for k in range(0, KEYS, KC):
            dp = dot_nt(kb[k:k + KC, 0:LAT], do)
            p = jnp.exp2(sv[k:k + KC, at] - top)
            pt[k:k + KC, at] = p.astype(BF16)
            dst[k:k + KC, at] = (p * (dp - rowdot)).astype(BF16)
            heads = p[:, 0:QT]
            for h in range(QT, R, QT):
                heads = heads + p[:, h:h + QT]
            masst[k:k + KC, :] += heads

    loop(0, ROWS // R, attend)

    for k in range(0, KEYS, KC):
        massq[:, k:k + KC] = masst[k:k + KC, :].T

    def mass_pair(i):
        send(rows(massq, 2 * i + (1 - c), QL), mcr.at[i], m_ss.at[i], m_rs.at[i], me_k, mate)

    loop(0, NZ, mass_pair)

    def at_step(i):
        return lax.rem(z + jnp.where(i == 0, 2, jnp.where(i == 1, 1, jnp.where(i == 2, 3, 0))), NZ)

    def key_group(g):
        base = g * 512
        lo = g * GW

        def finish(i):
            there = at_step(i)
            arrived(gcr.at[g, there], g_ss.at[g, there], g_rs.at[g, there])
            own_half = gown[pl.ds(pl.multiple_of(base + c * CH, CH), CH), span(i, GW)]
            gzs[g, there] = (own_half + gcr[g, there].astype(F32)).astype(BF16)
            send(gzs.at[g, there], gzr.at[g, z], gz_ss.at[g, there], gz_rs.at[g, z], me_k, there * 2 + c)

        def step(i):
            there = at_step(i)
            at = span(there, 2 * CH)
            lane = span(i, GW)
            if g < 2:
                gown[base:base + 512, lane] = (
                    dot_nt(dst[at, :], qt[lo:lo + GW, :]) * ATTN_SCALE + dot(pt[at, :], dov[:, lo:lo + GW])
                )
            else:
                rope = dot_nt(dst[at, :], qt[LAT:KD, :]) * ATTN_SCALE
                gown[base:base + 512, lane] = jnp.concatenate(
                    [rope, jnp.zeros((2 * CH, 128 - KD + LAT), F32), masst[at, :]], axis=1
                )
            gs[g, there] = gown[pl.ds(pl.multiple_of(base + (1 - c) * CH, CH), CH), lane].astype(BF16)
            send(gs.at[g, there], gcr.at[g, there], g_ss.at[g, there], g_rs.at[g, there], me_k, mate)

            @pl.when(i >= 1)
            def _():
                finish(i - 1)

        loop(0, NZ, step)

    def ship_home(g):
        arrived(gcr.at[g, z], g_ss.at[g, z], g_rs.at[g, z])
        acc = gown[pl.ds(pl.multiple_of(g * 512 + c * CH, CH), CH), 3 * GW:4 * GW] + gcr[g, z].astype(F32)
        for other in (zp, zm, zo):
            arrived(gzr.at[g, other], gz_ss.at[g, other], gz_rs.at[g, other])
            acc = acc + gzr[g, other].astype(F32)
        ob[g] = dot(to_slot[...], acc.astype(BF16)).astype(BF16)
        loop(1, NK, lambda d: send(
            home_part(ob, g, peer_k(d)), home_part(orx, g, me_k), o_ss.at[g, d], o_rs.at[g, d], peer_k(d), me_s))
        own = span(me_k, CAP * SUB)
        orx[g, own, :] = ob[g, own, :]

    def home_part(ref, g, k):
        return ref.at[g, span(k, CAP * SUB), :]

    key_group(0)
    def mass_sum(d):
        there = lax.rem(z + d, NZ)
        arrived(mcr.at[there], m_ss.at[there], m_rs.at[there])
        return massq[span(2 * there + c, QL), :] + mcr[there]

    for d in (2, 1, 3):
        mzs[d] = mass_sum(d)
        send(mzs.at[d], mzr.at[d], mz_ss.at[d], mz_rs.at[d], me_k, lax.rem(z + d, NZ) * 2 + c)
    mzs[0] = mass_sum(0)

    key_group(1)
    ship_home(0)

    logits = lgv[...]
    e = jnp.exp(logits - jnp.max(logits, axis=1, keepdims=True))
    guess = e / jnp.sum(e, axis=1, keepdims=True)
    mass = mzs[0]
    for d in (1, 2, 3):
        arrived(mzr.at[d], mz_ss.at[d], mz_rs.at[d])
        mass = mass + mzr[d]
    dlogit = INDEX_SCALE * (guess - mass * (1.0 / H))
    dlv[...] = jnp.broadcast_to(dlogit[:, None, :], (QL, JL, KEYS)).reshape(QJ, KEYS)
    ikt[...] = jnp.zeros(ikt.shape, F32)

    def index_part(src):
        sim = dot_nt(iqr[src], kb[:, IO:W])
        dl = dlv[...]
        ds = jnp.where(sim > 0, dl * jnp.tile(wv[src], (1, KEYS // 128)), 0.0).astype(BF16)
        dw = jnp.sum(dl * jnp.maximum(sim, 0.0), axis=1, keepdims=True).reshape(QL, JL, 1)
        diws[src] = jnp.sum(jnp.where(my_query, dw, 0.0), axis=0)
        diqs[span(src, QJ), :] = dot(ds, kb[:, IO:W])
        ikt[...] += dot(iqt[:, span(src, 128)], ds)

    loop(0, NS, index_part)

    def ship_grads(d):
        there = peer_s(d)
        send(rows(diqs, there, QJ), rows(diq_out, me_s, QJ), b_ss.at[d], b_rs.at[d], me_k, there)
        send(diws.at[there], diwr.at[me_s], v_ss.at[d], v_rs.at[d], me_k, there)

    loop(1, NS, ship_grads)
    diwr[me_s] = diws[me_s]
    here_iq = pltpu.make_async_copy(rows(diqs, me_s, QJ), rows(diq_out, me_s, QJ), fin_sem.at[0])
    here_iq.start()

    for k in range(0, KEYS, KC):
        masst[k:k + KC, :] = ikt[:, k:k + KC].T

    ship_home(1)
    key_group(2)

    def dq_copy(head):
        step = lax.div(head, 4)
        lane = span(lax.rem(head, 4), QT)
        return pltpu.make_async_copy(dqv.at[lax.rem(step, 2), :, lane], dq_out.at[head], dq_sem.at[head])

    def query_grad(step):
        at = span(step, 512)
        grad = (dot_tn(kb[:, 0:KD], dst[:, at]) * ATTN_SCALE).astype(BF16)

        @pl.when(step >= 2)
        def _():
            for h in range(4):
                dq_copy((step - 2) * 4 + h).wait()

        dqv[lax.rem(step, 2)] = grad
        for h in range(4):
            dq_copy(step * 4 + h).start()

    loop(0, 2, query_grad)
    ship_home(2)
    loop(2, 4, query_grad)

    def grads_here(d):
        arrived(rows(diq_out, from_s(d), QJ), b_ss.at[d], b_rs.at[d])
        arrived(diwr.at[from_s(d)], v_ss.at[d], v_rs.at[d])

    loop(1, NS, grads_here)
    weight_grad = diwr[0]
    for src in range(1, NS):
        weight_grad = weight_grad + diwr[src]
    diw_v[...] = weight_grad
    out_iw = pltpu.make_async_copy(diw_v, diw_out, fin_sem.at[1])
    out_iw.start()

    def sent_s(d):
        gone(rows(iq_hbm, peer_s(d), QJ), iqr.at[me_s], iq_ss.at[d], iq_rs.at[d])
        gone(iw_hbm, iwr.at[me_s], iw_ss.at[d], iw_rs.at[d])
        gone(rows(diqs, peer_s(d), QJ), rows(diq_out, me_s, QJ), b_ss.at[d], b_rs.at[d])
        gone(diws.at[peer_s(d)], diwr.at[me_s], v_ss.at[d], v_rs.at[d])

    loop(1, NS, sent_s)
    for lane, chunk in lanes.items():
        gone(rows(kb, chunk, CH), rows(kb, chunk, CH), ag_ss.at[lane], ag_rs.at[0])
    loop(1, NK, lambda d: gone(slots(sendb, peer_k(d)), slots(recvb, me_k), xs_ss.at[d], xs_rs.at[d]))

    def sent_pair(i):
        gone(rows(massq, 2 * i + (1 - c), QL), mcr.at[i], m_ss.at[i], m_rs.at[i])
        for g in range(GROUPS):
            gone(gs.at[g, i], gcr.at[g, i], g_ss.at[g, i], g_rs.at[g, i])

    loop(0, NZ, sent_pair)
    for d in (1, 2, 3):
        there = lax.rem(z + d, NZ)
        gone(mzs.at[d], mzr.at[d], mz_ss.at[d], mz_rs.at[d])
        for g in range(GROUPS):
            gone(gzs.at[g, there], gzr.at[g, z], gz_ss.at[g, there], gz_rs.at[g, z])

    loop(HL // 2, HL, lambda h: dq_copy(h).wait())
    here_iq.wait()
    out_iw.wait()

    for g in range(GROUPS):
        loop(1, NK, lambda d: arrived(home_part(orx, g, from_k(d)), o_ss.at[g, d], o_rs.at[g, d]))
        grads = dot_tn(to_block[...], orx[g])
        if g < 2:
            dlat_v[:, :, g * GW:(g + 1) * GW] = grads.reshape(NK, SUB, GW)
        else:
            dlat_v[:, :, LAT:KD] = grads[:, 0:KD - LAT].reshape(NK, SUB, KD - LAT)
            didx_v[...] = grads[:, GW - ID:GW].reshape(NK, SUB, ID)
    out_lat = pltpu.make_async_copy(dlat_v, dlat_out, fin_sem.at[2])
    out_lat.start()
    out_idx = pltpu.make_async_copy(didx_v, didx_out, fin_sem.at[3])
    out_idx.start()
    for g in range(GROUPS):
        loop(1, NK, lambda d: gone(
            home_part(ob, g, peer_k(d)), home_part(orx, g, me_k), o_ss.at[g, d], o_rs.at[g, d]))
    out_lat.wait()
    out_idx.wait()


def body(queries, out_grad, latent_keys, index_queries, index_weights, index_keys, picks):
    hbm = pl.BlockSpec(memory_space=pl.ANY)
    dma = pltpu.SemaphoreType.DMA
    v = pltpu.VMEM
    outs = pl.pallas_call(
        kernel,
        out_shape=[
            jax.ShapeDtypeStruct((HL, KD, QT), BF16),
            jax.ShapeDtypeStruct((NK, SUB, KD), F32),
            jax.ShapeDtypeStruct((QT * JL, ID), F32),
            jax.ShapeDtypeStruct((JL, QT), F32),
            jax.ShapeDtypeStruct((NK, SUB, ID), F32),
        ],
        in_specs=[hbm] * 6 + [pl.BlockSpec(memory_space=pltpu.SMEM)],
        out_specs=[hbm] * 5,
        scratch_shapes=[
            v((KD, ROWS), BF16), v((ROWS, LAT), BF16),
            v((NK, SUB, ID), BF16), v((NK, SUB, W), BF16),
            v((SLOTS, SUB, W), BF16), v((SLOTS, SUB, W), BF16), v((KEYS, W), BF16),
            v((SLOTS * SUB, CH), BF16), v((SLOTS * SUB, CH), BF16),
            v((KEYS, ROWS), F32),
            v((KEYS, ROWS), BF16), v((KEYS, ROWS), BF16), v((2, KD, 512), BF16), v((8, ROWS), F32),
            v((8, ROWS), F32), v((8, ROWS), F32),
            v((NS, QJ, ID), BF16), v((NS, JL, QT), F32), v((NS, QJ, 128), F32), v((QL, KEYS), F32),
            v((KEYS, QT), F32),
            v((NZ, QL, KEYS), F32), v((NZ, QL, KEYS), F32), v((NZ, QL, KEYS), F32),
            v((ID, NS * QJ), BF16), v((NS, JL, QT), F32), v((NS, JL, QT), F32),
            v((GROUPS, NZ, CH, GW), BF16), v((GROUPS, NZ, CH, GW), BF16),
            v((GROUPS, NZ, CH, GW), BF16), v((GROUPS, NZ, CH, GW), BF16),
            v((GROUPS, SLOTS * SUB, GW), BF16), v((GROUPS, SLOTS * SUB, GW), BF16),
            v((NK, SUB, KD), F32), v((NK, SUB, ID), F32), v((JL, QT), F32),
            pltpu.SMEM((NK, CAP), jnp.int32),
            dma((4,)), dma((HL,)), dma((NK,)), dma((NS,)), dma((NS,)), dma((NS,)), dma((NS,)),
            dma((NK,)), dma((NK,)), dma((NS,)), dma((NS,)), dma((HL,)),
            dma((NZ,)), dma((NZ,)), dma((NZ,)), dma((NZ,)),
            dma((GROUPS, NZ)), dma((GROUPS, NZ)), dma((GROUPS, NZ)), dma((GROUPS, NZ)),
            dma((GROUPS, NK)), dma((GROUPS, NK)), dma((NS,)), dma((NS,)), dma((NS,)), dma((NS,)), dma((4,)),
        ],
        compiler_params=pltpu.CompilerParams(
            collective_id=0, has_side_effects=True, vmem_limit_bytes=64 * 1024 * 1024
        ),
        name="sparse_attention_backward",
    )(
        queries.transpose(1, 2, 0),
        out_grad.reshape(ROWS, LAT),
        latent_keys.transpose(0, 2, 1),
        index_queries.reshape(QT * JL, ID),
        index_weights.T,
        index_keys,
        picks,
    )
    def hand_over(*refs):
        given, made, held, sems = refs[:5], refs[5:10], refs[10:15], refs[15]
        parts = []
        for i in range(5):
            count = 4 if i == 0 else 1
            size = given[i].shape[0] // count
            parts += [(i, pl.ds(n * size, size)) for n in range(count)]
        loads = [pltpu.make_async_copy(given[i].at[at], held[i].at[at], sems.at[n]) for n, (i, at) in enumerate(parts)]
        stores = [pltpu.make_async_copy(held[i].at[at], made[i].at[at], sems.at[n]) for n, (i, at) in enumerate(parts)]
        for load in loads:
            load.start()
        for load, store in zip(loads, stores):
            load.wait()
            store.start()
        for store in stores:
            store.wait()

    dq, dlat, diq, diw, didx = pl.pallas_call(
        hand_over,
        out_shape=[jax.ShapeDtypeStruct(o.shape, o.dtype) for o in outs],
        in_specs=[hbm] * 5,
        out_specs=[hbm] * 5,
        scratch_shapes=[v(o.shape, o.dtype) for o in outs] + [dma((8,))],
        compiler_params=pltpu.CompilerParams(vmem_limit_bytes=64 * 1024 * 1024),
        name="hand_over",
    )(*outs)
    return (dq.transpose(2, 0, 1), dlat, diq.reshape(QT, JL, ID), diw.T, didx)


def solution(mesh):
    placed = (
        P("sk", "sq", None),
        P("sk", "sq", None),
        P("sk", None, None),
        P("sk", "sq", None),
        P("sk", "sq"),
        P("sk", None, None),
        P(),
    )
    return jax.shard_map(
        body,
        mesh=mesh,
        in_specs=placed,
        out_specs=(
            P("sk", "sq", None),
            P("sk", "sq", None),
            P("sk", "sq", None),
            P("sk", "sq"),
            P("sk", "sq", None),
        ),
        check_vma=False,
    )
```

time: 543 us -> 103 us (0.19)
  waiting for transfers between devices: 262 us -> 0 us
  Pallas kernels: 0 us -> 102 us
  local copies, waits for them, and re-layouts: 95.7 us -> 0 us
  matrix products: 85.3 us -> 0 us
  other arithmetic: 55.5 us -> 0 us
  starting transfers between devices: 26.4 us -> 0 us
  between operations: 14.4 us -> 0.82 us
    all_to_all x4 -> x0, waiting for transfers between devices: 188 us -> none  [the longest x1 129 us: body(): lax.all_to_all(latent_slots, 'sk', split_axis=0, concat_axis=0, tiled=True)]
    pallas_call x0 -> x2, Pallas kernels: none -> 102 us  [the longest x1 99.2 us: body(): pl.pallas_call(kernel, out_shape=[jax.ShapeDtypeStruct((HL, KD, QT), BF16...]
    dot_general x10 -> x0, matrix products: 85.3 us -> none  [the longest x1 19.1 us: body(): jnp.einsum('qhk,qhv->kv', attn_probs.astype(jnp.bfloat16), out_grad, pref...]
    psum x1 -> x0, waiting for transfers between devices: 51 us -> none  [body(): logits, mass_total = lax.psum((partial_logit, head_mass), 'sq')]
    reshape x4 -> x0, local copies, waits for them, and re-layouts: 36.3 us -> none  [the longest x1 17.1 us: body(): latent_slots = jnp.zeros((slot_total, block_rows, key_width), jnp.float32...]
    all_to_all x4 -> x0, starting transfers between devices: 25.9 us -> none  [the longest x1 7.33 us: body(): lax.all_to_all(latent_slots, 'sk', split_axis=0, concat_axis=0, tiled=True)]
    reduce_scatter x2 -> x0, waiting for transfers between devices: 22.7 us -> none  [the longest x1 22.7 us: body(): lax.psum_scatter(densify(onehot, got_latent), 'sq', scatter_dimension=1,...]
    sub x1 -> x0, other arithmetic: 17.9 us -> none  [body(): attn_probs = jax.nn.softmax(scores, axis=-1)]
  transfers between devices with their start and end apart: 7 -> 0, of which waited for: 5 -> 0; matrix products, arithmetic and copies ran while one was open for 29% -> 0% of each run, Pallas kernels for 0% -> 0%
where the time goes in v2:
time: 103 us
  Pallas kernels  102 us (99%)
    pallas_call x1, Pallas kernels, body(): pl.pallas_call(kernel, out_shape=[jax.ShapeDtypeStruct((HL, KD, QT), BF16...  99.2 us
    pallas_call x1, Pallas kernels, body(): pl.pallas_call(hand_over, out_shape=[jax.ShapeDtypeStruct(o.shape, o.dtyp...  2.96 us

profile of v2, /device:TPU:0, one launch (start us, length us, event | category | flops | bytes accessed | tf_op | source)
XLA Modules:
  0.0 103.0 jit_solution(11441609234309795155)
XLA Ops:
  0.6 99.2 %sparse_attention_backward.1 = (bf16[16,576,128]{2,1,0:T(8,128)(2,1)}, f32[16,16,576]{2,1,0:T(8,128)}, f32[1024,128]{1,0:T(8,128)}, f32[8,128]{1,0:T(8,128)}, f32[16,16,128]{2,1,0:T(8,128)}) custom-call(bf16[16,576,128]{2,1,0:T(8,128)(2,1)} %bitcast.8, bf16[2048,512]{1,0:T(8,128)(2,1)} %bitcast.10, bf16[16,576,128]{2,1,0:T(8,128)(2,1)} %bitcast.9, ...), custom_call_target="tpu_custom_call" | custom-call | tf_op jit(solution)/shard_map/sparse_attention_backward/pallas_call | solution.py:527
  99.8 3.0 %hand_over.1 = (bf16[16,576,128]{2,1,0:T(8,128)(2,1)}, f32[16,16,576]{2,1,0:T(8,128)}, f32[1024,128]{1,0:T(8,128)}, f32[8,128]{1,0:T(8,128)}, f32[16,16,128]{2,1,0:T(8,128)}) custom-call(bf16[16,576,128]{2,1,0:T(8,128)(2,1)} %get-tuple-element.15.refs_0_, f32[16,16,576]{2,1,0:T(8,128)} %get-tuple-element.16.refs_1_, f32[1024,128]{1,0:T(8,128)} %get-tuple-element.17.refs_2_, ...), custom_call_target="tpu_custom_call" | custom-call | tf_op jit(solution)/shard_map/hand_over/pallas_call | solution.py:591

commit v3 on v2

--- a/solution.py
+++ b/solution.py
@@ -37,6 +37,7 @@
 SLOTS = NK * CAP
 W = 768
 IO = 640
+HALF = W // 2
 GW = 256
 GROUPS = 3
 R = 256
@@ -66,7 +67,7 @@
 def kernel(
     q_hbm, do_hbm, lat_hbm, iq_hbm, iw_hbm, idx_hbm, picks,
     dq_out, dlat_out, diq_out, diw_out, didx_out,
-    qt, dov, xi, xs, sendb, recvb, kb, to_slot, to_block, sv, pt, dst, dqv, topv, totv, dotv,
+    qt, dov, xi, xs, sendb, recv0, recv1, kb, to_slot, to_block, sv, pt, dst, dqv, topv, totv, dotv,
     iqr, iwr, wv, lgv, masst, mcr, mzs, mzr, iqt, diws, diwr,
     gs, gcr, gzs, gzr, ob, orx, dlat_v, didx_v, diw_v, found,
     ld_sem, q_sem, lat_sem, iq_ss, iq_rs, iw_ss, iw_rs, xs_ss, xs_rs, ag_ss, ag_rs, dq_sem,
@@ -176,18 +177,26 @@
         load.start()
 
     def pack(t):
-        sendb[2 * t] = xs[jnp.maximum(found[t, 0], 0)]
-        sendb[2 * t + 1] = xs[jnp.maximum(found[t, 1], 0)]
+        for i in range(CAP):
+            block = xs[jnp.maximum(found[t, i], 0)]
+            for f in range(2):
+                sendb[f, 2 * t + i] = block[:, f * HALF:(f + 1) * HALF]
 
     loop(0, NK, pack)
     pl.semaphore_wait(barrier, NK - 1 + NS - 1)
 
+    recvb = (recv0, recv1)
+
     def slots(ref, k):
         return ref.at[pl.ds(2 * k, 2)]
 
-    loop(1, NK, lambda d: send(
-        slots(sendb, peer_k(d)), slots(recvb, me_k), xs_ss.at[d], xs_rs.at[d], peer_k(d), me_s))
-    recvb[pl.ds(2 * me_k, 2)] = sendb[pl.ds(2 * me_k, 2)]
+    def fetch(f, d):
+        return remote(
+            slots(sendb.at[f], peer_k(d)), slots(recvb[f], me_k), xs_ss.at[f, d], xs_rs.at[f, d], peer_k(d), me_s)
+
+    for f in range(2):
+        loop(1, NK, lambda d: fetch(f, d).start())
+        recvb[f][pl.ds(2 * me_k, 2)] = sendb[f, pl.ds(2 * me_k, 2)]
 
     def ship_iq(d):
         send(rows(iq_hbm, peer_s(d), QJ), iqr.at[me_s], iq_ss.at[d], iq_rs.at[d], me_k, peer_s(d))
@@ -250,15 +259,28 @@
 
     fwd_from = jnp.where(c == 0, zm, zp)
     fwd_to = jnp.where(c == 0, zp, zm)
-    lanes = {}
     c2 = ATTN_SCALE * LOG2E
 
-    def pass_on(chunk, lane, sq):
-        lanes[lane] = chunk
-        send(rows(kb, chunk, CH), rows(kb, chunk, CH), ag_ss.at[lane], ag_rs.at[chunk], me_k, sq)
-
-    def chunk_here(chunk):
-        arrived(rows(kb, chunk, CH), ag_ss.at[0], ag_rs.at[chunk])
+    def chunk_ref(chunk, f):
+        return kb.at[span(chunk, CH), f * HALF:(f + 1) * HALF]
+
+    routes = (
+        (me_s, mate),
+        (me_s, fwd_to * 2 + c),
+        (me_s, fwd_from * 2 + c),
+        (fwd_from * 2 + c, fwd_to * 2 + c),
+        (fwd_from * 2 + c, mate),
+        (fwd_to * 2 + c, mate),
+        (zo * 2 + c, mate),
+    )
+
+    def pass_on(f, *which):
+        for lane in which:
+            chunk, sq = routes[lane]
+            send(chunk_ref(chunk, f), chunk_ref(chunk, f), ag_ss.at[f, lane], ag_rs.at[f, chunk], me_k, sq)
+
+    def chunk_here(f, chunk):
+        arrived(chunk_ref(chunk, f), ag_ss.at[f, 0], ag_rs.at[f, chunk])
 
     def meet(chunk):
         at = span(chunk, CH)
@@ -283,31 +305,56 @@
             acc = acc + jnp.maximum(dot_nt(iqr[src], keys), 0.0) * jnp.tile(wv[src], (1, CH // 128))
         lgv[:, at] = INDEX_SCALE * jnp.sum(acc.reshape(QL, JL, CH), axis=1)
 
-    def meet_mate(zz):
-        chunk_here(zz * 2 + (1 - c))
-        meet(zz * 2 + (1 - c))
-
-    loop(1, NK, lambda d: arrived(slots(recvb, from_k(d)), xs_ss.at[d], xs_rs.at[d]))
-    for p in range(PICKS):
-        kb[pl.ds(pl.multiple_of(me_s * CH + p * SUB, SUB), SUB), :] = recvb[slot[p]]
-    pass_on(me_s, 0, mate)
-    pass_on(me_s, 1, fwd_to * 2 + c)
-    meet(me_s)
-    pass_on(me_s, 2, fwd_from * 2 + c)
-    chunk_here(fwd_from * 2 + c)
-    pass_on(fwd_from * 2 + c, 3, fwd_to * 2 + c)
-    pass_on(fwd_from * 2 + c, 4, mate)
-    meet_mate(z)
-    meet(fwd_from * 2 + c)
-    chunk_here(fwd_to * 2 + c)
-    pass_on(fwd_to * 2 + c, 5, mate)
-    meet_mate(fwd_to)
-    meet(fwd_to * 2 + c)
-    chunk_here(zo * 2 + c)
-    pass_on(zo * 2 + c, 6, mate)
-    meet_mate(fwd_from)
-    meet(zo * 2 + c)
-    meet_mate(zo)
+    for f in range(2):
+        loop(1, NK, lambda d: fetch(f, d).wait_recv())
+        for p in range(PICKS):
+            kb[pl.ds(pl.multiple_of(me_s * CH + p * SUB, SUB), SUB), f * HALF:(f + 1) * HALF] = recvb[f][slot[p]]
+        pass_on(f, 0, 1, 2)
+
+    def via_from(f):
+        chunk_here(f, fwd_from * 2 + c)
+        pass_on(f, 3, 4)
+
+    def via_to(f):
+        chunk_here(f, fwd_to * 2 + c)
+        pass_on(f, 5)
+
+    def via_far(f):
+        chunk_here(f, zo * 2 + c)
+        pass_on(f, 6)
+
+    def gather_step(i):
+        side = jnp.where(
+            i < 2, z, jnp.where((i == 2) | (i == 5), fwd_from, jnp.where((i == 3) | (i == 4), fwd_to, zo))
+        )
+        own_core = lax.rem(i, 2) == 0
+
+        @pl.when(i == 1)
+        def _():
+            via_from(0)
+            via_to(0)
+
+        @pl.when(i == 2)
+        def _():
+            via_from(1)
+
+        @pl.when(i == 4)
+        def _():
+            via_to(1)
+            via_far(0)
+
+        @pl.when(i == 6)
+        def _():
+            via_far(1)
+
+        @pl.when(jnp.logical_not(own_core))
+        def _():
+            for f in range(2):
+                chunk_here(f, side * 2 + 1 - c)
+
+        meet(side * 2 + jnp.where(own_core, c, 1 - c))
+
+    loop(0, NS, gather_step)
 
     def attend(step):
         at = span(step, R)
@@ -338,9 +385,12 @@
     loop(0, NZ, mass_pair)
 
     def at_step(i):
-        return lax.rem(z + jnp.where(i == 0, 2, jnp.where(i == 1, 1, jnp.where(i == 2, 3, 0))), NZ)
-
-    def key_group(g):
+        return jnp.where(i == 0, zo, jnp.where(i == 1, fwd_from, jnp.where(i == 2, fwd_to, z)))
+
+    to_sq = fwd_to * 2 + c
+    from_sq = fwd_from * 2 + c
+
+    def key_group(g, then=None):
         base = g * 512
         lo = g * GW
 
@@ -348,8 +398,20 @@
             there = at_step(i)
             arrived(gcr.at[g, there], g_ss.at[g, there], g_rs.at[g, there])
             own_half = gown[pl.ds(pl.multiple_of(base + c * CH, CH), CH), span(i, GW)]
-            gzs[g, there] = (own_half + gcr[g, there].astype(F32)).astype(BF16)
-            send(gzs.at[g, there], gzr.at[g, z], gz_ss.at[g, there], gz_rs.at[g, z], me_k, there * 2 + c)
+            return own_half + gcr[g, there].astype(F32)
+
+        def relay():
+            gzs[g, 0] = finish(0).astype(BF16)
+            send(gzs.at[g, 0], gzr.at[g, 0], gz_ss.at[g, 0], gz_rs.at[g, 0], me_k, to_sq)
+
+        def back():
+            gzs[g, 1] = finish(1).astype(BF16)
+            send(gzs.at[g, 1], gzr.at[g, 1], gz_ss.at[g, 1], gz_rs.at[g, 1], me_k, from_sq)
+
+        def onward():
+            arrived(gzr.at[g, 0], gz_ss.at[g, 0], gz_rs.at[g, 0])
+            gzs[g, 2] = (finish(2) + gzr[g, 0].astype(F32)).astype(BF16)
+            send(gzs.at[g, 2], gzr.at[g, 2], gz_ss.at[g, 2], gz_rs.at[g, 2], me_k, to_sq)
 
         def step(i):
             there = at_step(i)
@@ -367,18 +429,19 @@
             gs[g, there] = gown[pl.ds(pl.multiple_of(base + (1 - c) * CH, CH), CH), lane].astype(BF16)
             send(gs.at[g, there], gcr.at[g, there], g_ss.at[g, there], g_rs.at[g, there], me_k, mate)
 
-            @pl.when(i >= 1)
-            def _():
-                finish(i - 1)
+            for n, act in ((1, relay), (2, back), (3, onward)):
+                pl.when(i == n)(act)
+            if then is not None:
+                pl.when(i == 1)(then)
 
         loop(0, NZ, step)
 
     def ship_home(g):
         arrived(gcr.at[g, z], g_ss.at[g, z], g_rs.at[g, z])
         acc = gown[pl.ds(pl.multiple_of(g * 512 + c * CH, CH), CH), 3 * GW:4 * GW] + gcr[g, z].astype(F32)
-        for other in (zp, zm, zo):
-            arrived(gzr.at[g, other], gz_ss.at[g, other], gz_rs.at[g, other])
-            acc = acc + gzr[g, other].astype(F32)
+        for way in (1, 2):
+            arrived(gzr.at[g, way], gz_ss.at[g, way], gz_rs.at[g, way])
+            acc = acc + gzr[g, way].astype(F32)
         ob[g] = dot(to_slot[...], acc.astype(BF16)).astype(BF16)
         loop(1, NK, lambda d: send(
             home_part(ob, g, peer_k(d)), home_part(orx, g, me_k), o_ss.at[g, d], o_rs.at[g, d], peer_k(d), me_s))
@@ -388,27 +451,31 @@
     def home_part(ref, g, k):
         return ref.at[g, span(k, CAP * SUB), :]
 
-    key_group(0)
-    def mass_sum(d):
-        there = lax.rem(z + d, NZ)
+    def mass_sum(there):
         arrived(mcr.at[there], m_ss.at[there], m_rs.at[there])
         return massq[span(2 * there + c, QL), :] + mcr[there]
 
-    for d in (2, 1, 3):
-        mzs[d] = mass_sum(d)
-        send(mzs.at[d], mzr.at[d], mz_ss.at[d], mz_rs.at[d], me_k, lax.rem(z + d, NZ) * 2 + c)
-    mzs[0] = mass_sum(0)
-
+    def mass_first():
+        mzs[0] = mass_sum(zo)
+        send(mzs.at[0], mzr.at[0], mz_ss.at[0], mz_rs.at[0], me_k, to_sq)
+        mzs[1] = mass_sum(fwd_from)
+        send(mzs.at[1], mzr.at[1], mz_ss.at[1], mz_rs.at[1], me_k, from_sq)
+
+    key_group(0, mass_first)
+    arrived(mzr.at[0], mz_ss.at[0], mz_rs.at[0])
+    mzs[2] = mass_sum(fwd_to) + mzr[0]
+    send(mzs.at[2], mzr.at[2], mz_ss.at[2], mz_rs.at[2], me_k, to_sq)
+    mzs[3] = mass_sum(z)
     key_group(1)
     ship_home(0)
 
     logits = lgv[...]
     e = jnp.exp(logits - jnp.max(logits, axis=1, keepdims=True))
     guess = e / jnp.sum(e, axis=1, keepdims=True)
-    mass = mzs[0]
-    for d in (1, 2, 3):
-        arrived(mzr.at[d], mz_ss.at[d], mz_rs.at[d])
-        mass = mass + mzr[d]
+    mass = mzs[3]
+    for way in (1, 2):
+        arrived(mzr.at[way], mz_ss.at[way], mz_rs.at[way])
+        mass = mass + mzr[way]
     dlogit = INDEX_SCALE * (guess - mass * (1.0 / H))
     dlv[...] = jnp.broadcast_to(dlogit[:, None, :], (QL, JL, KEYS)).reshape(QJ, KEYS)
     ikt[...] = jnp.zeros(ikt.shape, F32)
@@ -481,9 +548,10 @@
         gone(diws.at[peer_s(d)], diwr.at[me_s], v_ss.at[d], v_rs.at[d])
 
     loop(1, NS, sent_s)
-    for lane, chunk in lanes.items():
-        gone(rows(kb, chunk, CH), rows(kb, chunk, CH), ag_ss.at[lane], ag_rs.at[0])
-    loop(1, NK, lambda d: gone(slots(sendb, peer_k(d)), slots(recvb, me_k), xs_ss.at[d], xs_rs.at[d]))
+    for f in range(2):
+        for lane, (chunk, _) in enumerate(routes):
+            gone(chunk_ref(chunk, f), chunk_ref(chunk, f), ag_ss.at[f, lane], ag_rs.at[f, 0])
+        loop(1, NK, lambda d: fetch(f, d).wait_send())
 
     def sent_pair(i):
         gone(rows(massq, 2 * i + (1 - c), QL), mcr.at[i], m_ss.at[i], m_rs.at[i])
@@ -491,11 +559,10 @@
             gone(gs.at[g, i], gcr.at[g, i], g_ss.at[g, i], g_rs.at[g, i])
 
     loop(0, NZ, sent_pair)
-    for d in (1, 2, 3):
-        there = lax.rem(z + d, NZ)
-        gone(mzs.at[d], mzr.at[d], mz_ss.at[d], mz_rs.at[d])
+    for way in range(3):
+        gone(mzs.at[way], mzr.at[way], mz_ss.at[way], mz_rs.at[way])
         for g in range(GROUPS):
-            gone(gzs.at[g, there], gzr.at[g, z], gz_ss.at[g, there], gz_rs.at[g, z])
+            gone(gzs.at[g, way], gzr.at[g, way], gz_ss.at[g, way], gz_rs.at[g, way])
 
     loop(HL // 2, HL, lambda h: dq_copy(h).wait())
     here_iq.wait()
@@ -538,7 +605,8 @@
         scratch_shapes=[
             v((KD, ROWS), BF16), v((ROWS, LAT), BF16),
             v((NK, SUB, ID), BF16), v((NK, SUB, W), BF16),
-            v((SLOTS, SUB, W), BF16), v((SLOTS, SUB, W), BF16), v((KEYS, W), BF16),
+            v((2, SLOTS, SUB, HALF), BF16), v((SLOTS, SUB, HALF), BF16), v((SLOTS, SUB, HALF), BF16),
+            v((KEYS, W), BF16),
             v((SLOTS * SUB, CH), BF16), v((SLOTS * SUB, CH), BF16),
             v((KEYS, ROWS), F32),
             v((KEYS, ROWS), BF16), v((KEYS, ROWS), BF16), v((2, KD, 512), BF16), v((8, ROWS), F32),
@@ -553,7 +621,7 @@
             v((NK, SUB, KD), F32), v((NK, SUB, ID), F32), v((JL, QT), F32),
             pltpu.SMEM((NK, CAP), jnp.int32),
             dma((4,)), dma((HL,)), dma((NK,)), dma((NS,)), dma((NS,)), dma((NS,)), dma((NS,)),
-            dma((NK,)), dma((NK,)), dma((NS,)), dma((NS,)), dma((HL,)),
+            dma((2, NK)), dma((2, NK)), dma((2, NS)), dma((2, NS)), dma((HL,)),
             dma((NZ,)), dma((NZ,)), dma((NZ,)), dma((NZ,)),
             dma((GROUPS, NZ)), dma((GROUPS, NZ)), dma((GROUPS, NZ)), dma((GROUPS, NZ)),
             dma((GROUPS, NK)), dma((GROUPS, NK)), dma((NS,)), dma((NS,)), dma((NS,)), dma((NS,)), dma((4,)),

time: 103 us -> 97.7 us (0.949)
  Pallas kernels: 102 us -> 96.9 us
    pallas_call x1, Pallas kernels: 99.2 us -> 93.9 us  [body(): pl.pallas_call(kernel, out_shape=[jax.ShapeDtypeStruct((HL, KD, QT), BF16...]
where the time goes in v3:
time: 97.7 us; the launch traced here: 97.5 us
  Pallas kernels  96.9 us (99%)
    pallas_call x1, Pallas kernels, body(): pl.pallas_call(kernel, out_shape=[jax.ShapeDtypeStruct((HL, KD, QT), BF16...  93.9 us
    pallas_call x1, Pallas kernels, body(): pl.pallas_call(hand_over, out_shape=[jax.ShapeDtypeStruct(o.shape, o.dtyp...  2.96 us

profile of v3, /device:TPU:0, one launch (start us, length us, event | category | flops | bytes accessed | tf_op | source)
XLA Modules:
  0.0 97.5 jit_solution(11454297277250308764)
XLA Ops:
  0.6 93.9 %sparse_attention_backward.1 = (bf16[16,576,128]{2,1,0:T(8,128)(2,1)}, f32[16,16,576]{2,1,0:T(8,128)}, f32[1024,128]{1,0:T(8,128)}, f32[8,128]{1,0:T(8,128)}, f32[16,16,128]{2,1,0:T(8,128)}) custom-call(bf16[16,576,128]{2,1,0:T(8,128)(2,1)} %bitcast.8, bf16[2048,512]{1,0:T(8,128)(2,1)} %bitcast.10, bf16[16,576,128]{2,1,0:T(8,128)(2,1)} %bitcast.9, ...), custom_call_target="tpu_custom_call" | custom-call | tf_op jit(solution)/shard_map/sparse_attention_backward/pallas_call | solution.py:594
  94.5 3.0 %hand_over.1 = (bf16[16,576,128]{2,1,0:T(8,128)(2,1)}, f32[16,16,576]{2,1,0:T(8,128)}, f32[1024,128]{1,0:T(8,128)}, f32[8,128]{1,0:T(8,128)}, f32[16,16,128]{2,1,0:T(8,128)}) custom-call(bf16[16,576,128]{2,1,0:T(8,128)(2,1)} %get-tuple-element.15.refs_0_, f32[16,16,576]{2,1,0:T(8,128)} %get-tuple-element.16.refs_1_, f32[1024,128]{1,0:T(8,128)} %get-tuple-element.17.refs_2_, ...), custom_call_target="tpu_custom_call" | custom-call | tf_op jit(solution)/shard_map/hand_over/pallas_call | solution.py:659

commit v4 on v3

--- a/solution.py
+++ b/solution.py
@@ -67,7 +67,7 @@
 def kernel(
     q_hbm, do_hbm, lat_hbm, iq_hbm, iw_hbm, idx_hbm, picks,
     dq_out, dlat_out, diq_out, diw_out, didx_out,
-    qt, dov, xi, xs, sendb, recv0, recv1, kb, to_slot, to_block, sv, pt, dst, dqv, topv, totv, dotv,
+    qt, dov, xi, xs, sendb, recv0, recv1, kb, to_slot, to_block, home, sv, pt, dst, dqv, topv, totv, dotv,
     iqr, iwr, wv, lgv, masst, mcr, mzs, mzr, iqt, diws, diwr,
     gs, gcr, gzs, gzr, ob, orx, dlat_v, didx_v, diw_v, found,
     ld_sem, q_sem, lat_sem, iq_ss, iq_rs, iw_ss, iw_rs, xs_ss, xs_rs, ag_ss, ag_rs, dq_sem,
@@ -225,6 +225,7 @@
 
     loop(0, SLOTS, unpick)
     loop(0, NK, place)
+    home[...] = to_block[...].T
     i0, i1 = iota((CH, CH), 0), iota((CH, CH), 1)
     swap = ones_where(i1 == lax.rem(i0, 16) * 16 + lax.div(i0, 16))
     load_do.wait()
@@ -390,55 +391,50 @@
     to_sq = fwd_to * 2 + c
     from_sq = fwd_from * 2 + c
 
-    def key_group(g, then=None):
-        base = g * 512
-        lo = g * GW
-
-        def finish(i):
-            there = at_step(i)
-            arrived(gcr.at[g, there], g_ss.at[g, there], g_rs.at[g, there])
-            own_half = gown[pl.ds(pl.multiple_of(base + c * CH, CH), CH), span(i, GW)]
-            return own_half + gcr[g, there].astype(F32)
-
-        def relay():
-            gzs[g, 0] = finish(0).astype(BF16)
-            send(gzs.at[g, 0], gzr.at[g, 0], gz_ss.at[g, 0], gz_rs.at[g, 0], me_k, to_sq)
-
-        def back():
-            gzs[g, 1] = finish(1).astype(BF16)
-            send(gzs.at[g, 1], gzr.at[g, 1], gz_ss.at[g, 1], gz_rs.at[g, 1], me_k, from_sq)
-
-        def onward():
-            arrived(gzr.at[g, 0], gz_ss.at[g, 0], gz_rs.at[g, 0])
-            gzs[g, 2] = (finish(2) + gzr[g, 0].astype(F32)).astype(BF16)
-            send(gzs.at[g, 2], gzr.at[g, 2], gz_ss.at[g, 2], gz_rs.at[g, 2], me_k, to_sq)
-
-        def step(i):
-            there = at_step(i)
-            at = span(there, 2 * CH)
-            lane = span(i, GW)
-            if g < 2:
-                gown[base:base + 512, lane] = (
-                    dot_nt(dst[at, :], qt[lo:lo + GW, :]) * ATTN_SCALE + dot(pt[at, :], dov[:, lo:lo + GW])
-                )
-            else:
-                rope = dot_nt(dst[at, :], qt[LAT:KD, :]) * ATTN_SCALE
-                gown[base:base + 512, lane] = jnp.concatenate(
-                    [rope, jnp.zeros((2 * CH, 128 - KD + LAT), F32), masst[at, :]], axis=1
-                )
-            gs[g, there] = gown[pl.ds(pl.multiple_of(base + (1 - c) * CH, CH), CH), lane].astype(BF16)
-            send(gs.at[g, there], gcr.at[g, there], g_ss.at[g, there], g_rs.at[g, there], me_k, mate)
-
-            for n, act in ((1, relay), (2, back), (3, onward)):
-                pl.when(i == n)(act)
-            if then is not None:
-                pl.when(i == 1)(then)
-
-        loop(0, NZ, step)
+    def group_rows(g):
+        return span(g, 2 * CH)
+
+    def to_mate(g, i, grads):
+        there = at_step(i)
+        gown[group_rows(g), span(i, GW)] = grads
+        gs[g, there] = gown[span(2 * g + 1 - c, CH), span(i, GW)].astype(BF16)
+        send(gs.at[g, there], gcr.at[g, there], g_ss.at[g, there], g_rs.at[g, there], me_k, mate)
+
+    def key_part(n):
+        g, i = lax.div(n, NZ), lax.rem(n, NZ)
+        at = span(at_step(i), 2 * CH)
+        part = span(g, GW)
+        to_mate(g, i, dot_nt(dst[at, :], qt[part, :]) * ATTN_SCALE + dot(pt[at, :], dov[:, part]))
+
+    def rope_part(i):
+        at = span(at_step(i), 2 * CH)
+        rope = dot_nt(dst[at, :], qt[LAT:KD, :]) * ATTN_SCALE
+        empty = jnp.zeros((2 * CH, GW - ID - KD + LAT), F32)
+        to_mate(2, i, jnp.concatenate([rope, empty, masst[at, :]], axis=1))
+
+    def of_chip(g, i):
+        there = at_step(i)
+        arrived(gcr.at[g, there], g_ss.at[g, there], g_rs.at[g, there])
+        return gown[span(2 * g + c, CH), span(i, GW)] + gcr[g, there].astype(F32)
+
+    def along(g, way, sq):
+        send(gzs.at[g, way], gzr.at[g, way], gz_ss.at[g, way], gz_rs.at[g, way], me_k, sq)
+
+    def relay(g):
+        gzs[g, 0] = of_chip(g, 0).astype(BF16)
+        along(g, 0, to_sq)
+
+    def back(g):
+        gzs[g, 1] = of_chip(g, 1).astype(BF16)
+        along(g, 1, from_sq)
+
+    def onward(g):
+        arrived(gzr.at[g, 0], gz_ss.at[g, 0], gz_rs.at[g, 0])
+        gzs[g, 2] = (of_chip(g, 2) + gzr[g, 0].astype(F32)).astype(BF16)
+        along(g, 2, to_sq)
 
     def ship_home(g):
-        arrived(gcr.at[g, z], g_ss.at[g, z], g_rs.at[g, z])
-        acc = gown[pl.ds(pl.multiple_of(g * 512 + c * CH, CH), CH), 3 * GW:4 * GW] + gcr[g, z].astype(F32)
+        acc = of_chip(g, 3)
         for way in (1, 2):
             arrived(gzr.at[g, way], gz_ss.at[g, way], gz_rs.at[g, way])
             acc = acc + gzr[g, way].astype(F32)
@@ -461,12 +457,22 @@
         mzs[1] = mass_sum(fwd_from)
         send(mzs.at[1], mzr.at[1], mz_ss.at[1], mz_rs.at[1], me_k, from_sq)
 
-    key_group(0, mass_first)
-    arrived(mzr.at[0], mz_ss.at[0], mz_rs.at[0])
-    mzs[2] = mass_sum(fwd_to) + mzr[0]
-    send(mzs.at[2], mzr.at[2], mz_ss.at[2], mz_rs.at[2], me_k, to_sq)
-    mzs[3] = mass_sum(z)
-    key_group(1)
+    def mass_onward():
+        arrived(mzr.at[0], mz_ss.at[0], mz_rs.at[0])
+        mzs[2] = mass_sum(fwd_to) + mzr[0]
+        send(mzs.at[2], mzr.at[2], mz_ss.at[2], mz_rs.at[2], me_k, to_sq)
+        mzs[3] = mass_sum(z)
+
+    def key_step(n):
+        key_part(n)
+        pl.when(n == 2)(mass_first)
+        for g in range(2):
+            for i, act in enumerate((relay, back, onward)):
+                pl.when(n == g * NZ + i + 2)(lambda g=g, act=act: act(g))
+        pl.when(n == 6)(mass_onward)
+
+    loop(0, 2 * NZ, key_step)
+    onward(1)
     ship_home(0)
 
     logits = lgv[...]
@@ -505,7 +511,7 @@
         masst[k:k + KC, :] = ikt[:, k:k + KC].T
 
     ship_home(1)
-    key_group(2)
+    loop(0, NZ, rope_part)
 
     def dq_copy(head):
         step = lax.div(head, 4)
@@ -525,9 +531,18 @@
         for h in range(4):
             dq_copy(step * 4 + h).start()
 
-    loop(0, 2, query_grad)
-    ship_home(2)
-    loop(2, 4, query_grad)
+    def last_step(i):
+        query_grad(i)
+
+        @pl.when(i == 0)
+        def _():
+            relay(2)
+            back(2)
+
+        pl.when(i == 1)(lambda: onward(2))
+        pl.when(i == 2)(lambda: ship_home(2))
+
+    loop(0, 4, last_step)
 
     def grads_here(d):
         arrived(rows(diq_out, from_s(d), QJ), b_ss.at[d], b_rs.at[d])
@@ -570,7 +585,7 @@
 
     for g in range(GROUPS):
         loop(1, NK, lambda d: arrived(home_part(orx, g, from_k(d)), o_ss.at[g, d], o_rs.at[g, d]))
-        grads = dot_tn(to_block[...], orx[g])
+        grads = dot(home[...], orx[g])
         if g < 2:
             dlat_v[:, :, g * GW:(g + 1) * GW] = grads.reshape(NK, SUB, GW)
         else:
@@ -607,7 +622,7 @@
             v((NK, SUB, ID), BF16), v((NK, SUB, W), BF16),
             v((2, SLOTS, SUB, HALF), BF16), v((SLOTS, SUB, HALF), BF16), v((SLOTS, SUB, HALF), BF16),
             v((KEYS, W), BF16),
-            v((SLOTS * SUB, CH), BF16), v((SLOTS * SUB, CH), BF16),
+            v((SLOTS * SUB, CH), BF16), v((SLOTS * SUB, CH), BF16), v((CH, SLOTS * SUB), BF16),
             v((KEYS, ROWS), F32),
             v((KEYS, ROWS), BF16), v((KEYS, ROWS), BF16), v((2, KD, 512), BF16), v((8, ROWS), F32),
             v((8, ROWS), F32), v((8, ROWS), F32),

time: 97.7 us -> 99.5 us (1.018)
  Pallas kernels: 96.9 us -> 98.7 us
    pallas_call x1, Pallas kernels: 93.9 us -> 95.7 us  [body(): pl.pallas_call(kernel, out_shape=[jax.ShapeDtypeStruct((HL, KD, QT), BF16...]
where the time goes in v4:
time: 99.5 us; the launch traced here: 99.3 us
  Pallas kernels  98.7 us (99%)
    pallas_call x1, Pallas kernels, body(): pl.pallas_call(kernel, out_shape=[jax.ShapeDtypeStruct((HL, KD, QT), BF16...  95.7 us
    pallas_call x1, Pallas kernels, body(): pl.pallas_call(hand_over, out_shape=[jax.ShapeDtypeStruct(o.shape, o.dtyp...  2.96 us

profile of v4, /device:TPU:0, one launch (start us, length us, event | category | flops | bytes accessed | tf_op | source)
XLA Modules:
  0.0 99.3 jit_solution(716786167228004314)
XLA Ops:
  0.6 95.7 %sparse_attention_backward.1 = (bf16[16,576,128]{2,1,0:T(8,128)(2,1)}, f32[16,16,576]{2,1,0:T(8,128)}, f32[1024,128]{1,0:T(8,128)}, f32[8,128]{1,0:T(8,128)}, f32[16,16,128]{2,1,0:T(8,128)}) custom-call(bf16[16,576,128]{2,1,0:T(8,128)(2,1)} %bitcast.8, bf16[2048,512]{1,0:T(8,128)(2,1)} %bitcast.10, bf16[16,576,128]{2,1,0:T(8,128)(2,1)} %bitcast.9, ...), custom_call_target="tpu_custom_call" | custom-call | tf_op jit(solution)/shard_map/sparse_attention_backward/pallas_call | solution.py:609
  96.4 3.0 %hand_over.1 = (bf16[16,576,128]{2,1,0:T(8,128)(2,1)}, f32[16,16,576]{2,1,0:T(8,128)}, f32[1024,128]{1,0:T(8,128)}, f32[8,128]{1,0:T(8,128)}, f32[16,16,128]{2,1,0:T(8,128)}) custom-call(bf16[16,576,128]{2,1,0:T(8,128)(2,1)} %get-tuple-element.15.refs_0_, f32[16,16,576]{2,1,0:T(8,128)} %get-tuple-element.16.refs_1_, f32[1024,128]{1,0:T(8,128)} %get-tuple-element.17.refs_2_, ...), custom_call_target="tpu_custom_call" | custom-call | tf_op jit(solution)/shard_map/hand_over/pallas_call | solution.py:674

commit v5 on v4

--- a/solution.py
+++ b/solution.py
@@ -391,32 +391,16 @@
     to_sq = fwd_to * 2 + c
     from_sq = fwd_from * 2 + c
 
-    def group_rows(g):
-        return span(g, 2 * CH)
-
-    def to_mate(g, i, grads):
-        there = at_step(i)
-        gown[group_rows(g), span(i, GW)] = grads
-        gs[g, there] = gown[span(2 * g + 1 - c, CH), span(i, GW)].astype(BF16)
-        send(gs.at[g, there], gcr.at[g, there], g_ss.at[g, there], g_rs.at[g, there], me_k, mate)
-
-    def key_part(n):
-        g, i = lax.div(n, NZ), lax.rem(n, NZ)
-        at = span(at_step(i), 2 * CH)
-        part = span(g, GW)
-        to_mate(g, i, dot_nt(dst[at, :], qt[part, :]) * ATTN_SCALE + dot(pt[at, :], dov[:, part]))
-
-    def rope_part(i):
-        at = span(at_step(i), 2 * CH)
-        rope = dot_nt(dst[at, :], qt[LAT:KD, :]) * ATTN_SCALE
-        empty = jnp.zeros((2 * CH, GW - ID - KD + LAT), F32)
-        to_mate(2, i, jnp.concatenate([rope, empty, masst[at, :]], axis=1))
-
     def of_chip(g, i):
         there = at_step(i)
         arrived(gcr.at[g, there], g_ss.at[g, there], g_rs.at[g, there])
         return gown[span(2 * g + c, CH), span(i, GW)] + gcr[g, there].astype(F32)
 
+    def to_mate(g, i):
+        there = at_step(i)
+        gs[g, there] = gown[span(2 * g + 1 - c, CH), span(i, GW)].astype(BF16)
+        send(gs.at[g, there], gcr.at[g, there], g_ss.at[g, there], g_rs.at[g, there], me_k, mate)
+
     def along(g, way, sq):
         send(gzs.at[g, way], gzr.at[g, way], gz_ss.at[g, way], gz_rs.at[g, way], me_k, sq)
 
@@ -433,9 +417,34 @@
         gzs[g, 2] = (of_chip(g, 2) + gzr[g, 0].astype(F32)).astype(BF16)
         along(g, 2, to_sq)
 
+    def key_group(g, acts):
+        lo = g * GW
+
+        def step(i):
+            at = span(at_step(i), 2 * CH)
+            gown[g * 512:(g + 1) * 512, span(i, GW)] = (
+                dot_nt(dst[at, :], qt[lo:lo + GW, :]) * ATTN_SCALE + dot(pt[at, :], dov[:, lo:lo + GW])
+            )
+            to_mate(g, i)
+            for n, act in acts:
+                pl.when(i == n)(act)
+
+        loop(0, NZ, step)
+
+    def rope_part(i):
+        at = span(at_step(i), 2 * CH)
+        rope = dot_nt(dst[at, :], qt[LAT:KD, :]) * ATTN_SCALE
+        lane = pl.ds(pl.multiple_of(i * GW, 128), 128)
+        gown[1024:1536, lane] = jnp.concatenate([rope, jnp.zeros((2 * CH, 128 - KD + LAT), F32)], axis=1)
+
+    def index_pair(i):
+        lane = pl.ds(pl.multiple_of(i * GW + 128, 128), 128)
+        gown[1024:1536, lane] = masst[span(at_step(i), 2 * CH), :]
+        to_mate(2, i)
+
     def ship_home(g):
         acc = of_chip(g, 3)
-        for way in (1, 2):
+        for way in (1, 2) if g < 2 else (0, 1, 2):
             arrived(gzr.at[g, way], gz_ss.at[g, way], gz_rs.at[g, way])
             acc = acc + gzr[g, way].astype(F32)
         ob[g] = dot(to_slot[...], acc.astype(BF16)).astype(BF16)
@@ -463,17 +472,30 @@
         send(mzs.at[2], mzr.at[2], mz_ss.at[2], mz_rs.at[2], me_k, to_sq)
         mzs[3] = mass_sum(z)
 
-    def key_step(n):
-        key_part(n)
-        pl.when(n == 2)(mass_first)
-        for g in range(2):
-            for i, act in enumerate((relay, back, onward)):
-                pl.when(n == g * NZ + i + 2)(lambda g=g, act=act: act(g))
-        pl.when(n == 6)(mass_onward)
-
-    loop(0, 2 * NZ, key_step)
+    def dq_copy(head):
+        step = lax.div(head, 4)
+        lane = span(lax.rem(head, 4), QT)
+        return pltpu.make_async_copy(dqv.at[lax.rem(step, 2), :, lane], dq_out.at[head], dq_sem.at[head])
+
+    def query_grad(step):
+        at = span(step, 512)
+        grad = (dot_tn(kb[:, 0:KD], dst[:, at]) * ATTN_SCALE).astype(BF16)
+
+        @pl.when(step >= 2)
+        def _():
+            for h in range(4):
+                dq_copy((step - 2) * 4 + h).wait()
+
+        dqv[lax.rem(step, 2)] = grad
+        for h in range(4):
+            dq_copy(step * 4 + h).start()
+
+    key_group(0, ((1, lambda: relay(0)), (2, lambda: back(0)), (3, mass_first)))
+    key_group(1, ((1, lambda: relay(1)), (1, lambda: onward(0)), (2, lambda: back(1)), (3, mass_onward)))
+    loop(0, NZ, rope_part)
     onward(1)
     ship_home(0)
+    loop(0, 1, query_grad)
 
     logits = lgv[...]
     e = jnp.exp(logits - jnp.max(logits, axis=1, keepdims=True))
@@ -510,39 +532,13 @@
     for k in range(0, KEYS, KC):
         masst[k:k + KC, :] = ikt[:, k:k + KC].T
 
+    loop(0, NZ, index_pair)
     ship_home(1)
-    loop(0, NZ, rope_part)
-
-    def dq_copy(head):
-        step = lax.div(head, 4)
-        lane = span(lax.rem(head, 4), QT)
-        return pltpu.make_async_copy(dqv.at[lax.rem(step, 2), :, lane], dq_out.at[head], dq_sem.at[head])
-
-    def query_grad(step):
-        at = span(step, 512)
-        grad = (dot_tn(kb[:, 0:KD], dst[:, at]) * ATTN_SCALE).astype(BF16)
-
-        @pl.when(step >= 2)
-        def _():
-            for h in range(4):
-                dq_copy((step - 2) * 4 + h).wait()
-
-        dqv[lax.rem(step, 2)] = grad
-        for h in range(4):
-            dq_copy(step * 4 + h).start()
-
-    def last_step(i):
-        query_grad(i)
-
-        @pl.when(i == 0)
-        def _():
-            relay(2)
-            back(2)
-
-        pl.when(i == 1)(lambda: onward(2))
-        pl.when(i == 2)(lambda: ship_home(2))
-
-    loop(0, 4, last_step)
+    for way, sq in ((0, zo * 2 + c), (1, from_sq), (2, to_sq)):
+        gzs[2, way] = of_chip(2, way).astype(BF16)
+        along(2, way, sq)
+    loop(1, 4, query_grad)
+    ship_home(2)
 
     def grads_here(d):
         arrived(rows(diq_out, from_s(d), QJ), b_ss.at[d], b_rs.at[d])

time: 99.5 us -> 97.8 us (0.983)
  Pallas kernels: 98.7 us -> 96.9 us
    pallas_call x1, Pallas kernels: 95.7 us -> 94 us  [body(): pl.pallas_call(kernel, out_shape=[jax.ShapeDtypeStruct((HL, KD, QT), BF16...]
where the time goes in v5:
time: 97.8 us; the launch traced here: 97.6 us
  Pallas kernels  96.9 us (99%)
    pallas_call x1, Pallas kernels, body(): pl.pallas_call(kernel, out_shape=[jax.ShapeDtypeStruct((HL, KD, QT), BF16...  94 us
    pallas_call x1, Pallas kernels, body(): pl.pallas_call(hand_over, out_shape=[jax.ShapeDtypeStruct(o.shape, o.dtyp...  2.96 us

profile of v5, /device:TPU:0, one launch (start us, length us, event | category | flops | bytes accessed | tf_op | source)
XLA Modules:
  0.0 97.6 jit_solution(10213912967308599673)
XLA Ops:
  0.6 94.0 %sparse_attention_backward.1 = (bf16[16,576,128]{2,1,0:T(8,128)(2,1)}, f32[16,16,576]{2,1,0:T(8,128)}, f32[1024,128]{1,0:T(8,128)}, f32[8,128]{1,0:T(8,128)}, f32[16,16,128]{2,1,0:T(8,128)}) custom-call(bf16[16,576,128]{2,1,0:T(8,128)(2,1)} %bitcast.8, bf16[2048,512]{1,0:T(8,128)(2,1)} %bitcast.10, bf16[16,576,128]{2,1,0:T(8,128)(2,1)} %bitcast.9, ...), custom_call_target="tpu_custom_call" | custom-call | tf_op jit(solution)/shard_map/sparse_attention_backward/pallas_call | solution.py:605
  94.6 3.0 %hand_over.1 = (bf16[16,576,128]{2,1,0:T(8,128)(2,1)}, f32[16,16,576]{2,1,0:T(8,128)}, f32[1024,128]{1,0:T(8,128)}, f32[8,128]{1,0:T(8,128)}, f32[16,16,128]{2,1,0:T(8,128)}) custom-call(bf16[16,576,128]{2,1,0:T(8,128)(2,1)} %get-tuple-element.15.refs_0_, f32[16,16,576]{2,1,0:T(8,128)} %get-tuple-element.16.refs_1_, f32[1024,128]{1,0:T(8,128)} %get-tuple-element.17.refs_2_, ...), custom_call_target="tpu_custom_call" | custom-call | tf_op jit(solution)/shard_map/hand_over/pallas_call | solution.py:670

commit v6 on v5

--- a/solution.py
+++ b/solution.py
@@ -39,7 +39,8 @@
 IO = 640
 HALF = W // 2
 GW = 256
-GROUPS = 3
+WIDTHS = (256, 256, 128, 128)
+GROUPS = len(WIDTHS)
 R = 256
 KC = 256
 
@@ -76,7 +77,7 @@
     massq = sv.at[0:QT]
     dlv = sv.at[QT:QT + QJ]
     ikt = sv.at[256:256 + ID]
-    gown = sv.at[512:512 + GROUPS * 512, 0:NZ * GW]
+    gown = sv.at[512:512 + 3 * 512, 0:NZ * GW]
     diqs = sv.at[512:512 + NS * QJ, NZ * GW:NZ * GW + ID]
 
     me_k = lax.axis_index("sk")
@@ -391,18 +392,30 @@
     to_sq = fwd_to * 2 + c
     from_sq = fwd_from * 2 + c
 
+    def spot(g, core, i):
+        rows_at = pl.ds(pl.multiple_of((2 * min(g, 2) + core) * CH, CH), CH)
+        return rows_at, pl.ds(pl.multiple_of(i * GW + (128 if g == 3 else 0), 128), WIDTHS[g])
+
+    def cut(ref, g, *at):
+        return ref.at[(g, *at, slice(None), slice(0, WIDTHS[g]))]
+
     def of_chip(g, i):
         there = at_step(i)
-        arrived(gcr.at[g, there], g_ss.at[g, there], g_rs.at[g, there])
-        return gown[span(2 * g + c, CH), span(i, GW)] + gcr[g, there].astype(F32)
+        arrived(cut(gcr, g, there), g_ss.at[g, there], g_rs.at[g, there])
+        return gown[spot(g, c, i)] + cut(gcr, g, there)[...].astype(F32)
 
     def to_mate(g, i):
         there = at_step(i)
-        gs[g, there] = gown[span(2 * g + 1 - c, CH), span(i, GW)].astype(BF16)
-        send(gs.at[g, there], gcr.at[g, there], g_ss.at[g, there], g_rs.at[g, there], me_k, mate)
+        cut(gs, g, there)[...] = gown[spot(g, 1 - c, i)].astype(BF16)
+        send(cut(gs, g, there), cut(gcr, g, there), g_ss.at[g, there], g_rs.at[g, there], me_k, mate)
 
     def along(g, way, sq):
-        send(gzs.at[g, way], gzr.at[g, way], gz_ss.at[g, way], gz_rs.at[g, way], me_k, sq)
+        send(cut(gzs, g, way), cut(gzr, g, way), gz_ss.at[g, way], gz_rs.at[g, way], me_k, sq)
+
+    def direct(g):
+        for way, sq in ((0, zo * 2 + c), (1, from_sq), (2, to_sq)):
+            cut(gzs, g, way)[...] = of_chip(g, way).astype(BF16)
+            along(g, way, sq)
 
     def relay(g):
         gzs[g, 0] = of_chip(g, 0).astype(BF16)
@@ -436,25 +449,27 @@
         rope = dot_nt(dst[at, :], qt[LAT:KD, :]) * ATTN_SCALE
         lane = pl.ds(pl.multiple_of(i * GW, 128), 128)
         gown[1024:1536, lane] = jnp.concatenate([rope, jnp.zeros((2 * CH, 128 - KD + LAT), F32)], axis=1)
+        to_mate(2, i)
 
     def index_pair(i):
         lane = pl.ds(pl.multiple_of(i * GW + 128, 128), 128)
         gown[1024:1536, lane] = masst[span(at_step(i), 2 * CH), :]
-        to_mate(2, i)
+        to_mate(3, i)
 
     def ship_home(g):
         acc = of_chip(g, 3)
         for way in (1, 2) if g < 2 else (0, 1, 2):
-            arrived(gzr.at[g, way], gz_ss.at[g, way], gz_rs.at[g, way])
-            acc = acc + gzr[g, way].astype(F32)
-        ob[g] = dot(to_slot[...], acc.astype(BF16)).astype(BF16)
+            arrived(cut(gzr, g, way), gz_ss.at[g, way], gz_rs.at[g, way])
+            acc = acc + cut(gzr, g, way)[...].astype(F32)
+        lanes = slice(0, WIDTHS[g])
+        ob[g, :, lanes] = dot(to_slot[...], acc.astype(BF16)).astype(BF16)
         loop(1, NK, lambda d: send(
             home_part(ob, g, peer_k(d)), home_part(orx, g, me_k), o_ss.at[g, d], o_rs.at[g, d], peer_k(d), me_s))
         own = span(me_k, CAP * SUB)
-        orx[g, own, :] = ob[g, own, :]
+        orx[g, own, lanes] = ob[g, own, lanes]
 
     def home_part(ref, g, k):
-        return ref.at[g, span(k, CAP * SUB), :]
+        return ref.at[g, span(k, CAP * SUB), 0:WIDTHS[g]]
 
     def mass_sum(there):
         arrived(mcr.at[there], m_ss.at[there], m_rs.at[there])
@@ -496,6 +511,7 @@
     onward(1)
     ship_home(0)
     loop(0, 1, query_grad)
+    direct(2)
 
     logits = lgv[...]
     e = jnp.exp(logits - jnp.max(logits, axis=1, keepdims=True))
@@ -516,6 +532,8 @@
         diws[src] = jnp.sum(jnp.where(my_query, dw, 0.0), axis=0)
         diqs[span(src, QJ), :] = dot(ds, kb[:, IO:W])
         ikt[...] += dot(iqt[:, span(src, 128)], ds)
+        pl.when(src == 3)(lambda: ship_home(1))
+        pl.when(src == 6)(lambda: ship_home(2))
 
     loop(0, NS, index_part)
 
@@ -533,12 +551,9 @@
         masst[k:k + KC, :] = ikt[:, k:k + KC].T
 
     loop(0, NZ, index_pair)
-    ship_home(1)
-    for way, sq in ((0, zo * 2 + c), (1, from_sq), (2, to_sq)):
-        gzs[2, way] = of_chip(2, way).astype(BF16)
-        along(2, way, sq)
+    direct(3)
     loop(1, 4, query_grad)
-    ship_home(2)
+    ship_home(3)
 
     def grads_here(d):
         arrived(rows(diq_out, from_s(d), QJ), b_ss.at[d], b_rs.at[d])
@@ -567,13 +582,13 @@
     def sent_pair(i):
         gone(rows(massq, 2 * i + (1 - c), QL), mcr.at[i], m_ss.at[i], m_rs.at[i])
         for g in range(GROUPS):
-            gone(gs.at[g, i], gcr.at[g, i], g_ss.at[g, i], g_rs.at[g, i])
+            gone(cut(gs, g, i), cut(gcr, g, i), g_ss.at[g, i], g_rs.at[g, i])
 
     loop(0, NZ, sent_pair)
     for way in range(3):
         gone(mzs.at[way], mzr.at[way], mz_ss.at[way], mz_rs.at[way])
         for g in range(GROUPS):
-            gone(gzs.at[g, way], gzr.at[g, way], gz_ss.at[g, way], gz_rs.at[g, way])
+            gone(cut(gzs, g, way), cut(gzr, g, way), gz_ss.at[g, way], gz_rs.at[g, way])
 
     loop(HL // 2, HL, lambda h: dq_copy(h).wait())
     here_iq.wait()
@@ -581,12 +596,13 @@
 
     for g in range(GROUPS):
         loop(1, NK, lambda d: arrived(home_part(orx, g, from_k(d)), o_ss.at[g, d], o_rs.at[g, d]))
-        grads = dot(home[...], orx[g])
+        grads = dot(home[...], orx[g, :, 0:WIDTHS[g]])
         if g < 2:
             dlat_v[:, :, g * GW:(g + 1) * GW] = grads.reshape(NK, SUB, GW)
+        elif g == 2:
+            dlat_v[:, :, LAT:KD] = grads[:, 0:KD - LAT].reshape(NK, SUB, KD - LAT)
         else:
-            dlat_v[:, :, LAT:KD] = grads[:, 0:KD - LAT].reshape(NK, SUB, KD - LAT)
-            didx_v[...] = grads[:, GW - ID:GW].reshape(NK, SUB, ID)
+            didx_v[...] = grads.reshape(NK, SUB, ID)
     out_lat = pltpu.make_async_copy(dlat_v, dlat_out, fin_sem.at[2])
     out_lat.start()
     out_idx = pltpu.make_async_copy(didx_v, didx_out, fin_sem.at[3])

time: 97.8 us -> 95.6 us (0.978)
  Pallas kernels: 96.9 us -> 94.8 us
    pallas_call x1, Pallas kernels: 94 us -> 91.8 us  [body(): pl.pallas_call(kernel, out_shape=[jax.ShapeDtypeStruct((HL, KD, QT), BF16...]
where the time goes in v6:
time: 95.6 us; the launch traced here: 95.4 us
  Pallas kernels  94.8 us (99%)
    pallas_call x1, Pallas kernels, body(): pl.pallas_call(kernel, out_shape=[jax.ShapeDtypeStruct((HL, KD, QT), BF16...  91.8 us
    pallas_call x1, Pallas kernels, body(): pl.pallas_call(hand_over, out_shape=[jax.ShapeDtypeStruct(o.shape, o.dtyp...  2.96 us

profile of v6, /device:TPU:0, one launch (start us, length us, event | category | flops | bytes accessed | tf_op | source)
XLA Modules:
  0.0 95.4 jit_solution(5547608169102369823)
XLA Ops:
  0.6 91.8 %sparse_attention_backward.1 = (bf16[16,576,128]{2,1,0:T(8,128)(2,1)}, f32[16,16,576]{2,1,0:T(8,128)}, f32[1024,128]{1,0:T(8,128)}, f32[8,128]{1,0:T(8,128)}, f32[16,16,128]{2,1,0:T(8,128)}) custom-call(bf16[16,576,128]{2,1,0:T(8,128)(2,1)} %bitcast.8, bf16[2048,512]{1,0:T(8,128)(2,1)} %bitcast.10, bf16[16,576,128]{2,1,0:T(8,128)(2,1)} %bitcast.9, ...), custom_call_target="tpu_custom_call" | custom-call | tf_op jit(solution)/shard_map/sparse_attention_backward/pallas_call | solution.py:621
  92.4 3.0 %hand_over.1 = (bf16[16,576,128]{2,1,0:T(8,128)(2,1)}, f32[16,16,576]{2,1,0:T(8,128)}, f32[1024,128]{1,0:T(8,128)}, f32[8,128]{1,0:T(8,128)}, f32[16,16,128]{2,1,0:T(8,128)}) custom-call(bf16[16,576,128]{2,1,0:T(8,128)(2,1)} %get-tuple-element.15.refs_0_, f32[16,16,576]{2,1,0:T(8,128)} %get-tuple-element.16.refs_1_, f32[1024,128]{1,0:T(8,128)} %get-tuple-element.17.refs_2_, ...), custom_call_target="tpu_custom_call" | custom-call | tf_op jit(solution)/shard_map/hand_over/pallas_call | solution.py:686

commit v7 on v6

--- a/solution.py
+++ b/solution.py
@@ -524,7 +524,13 @@
     dlv[...] = jnp.broadcast_to(dlogit[:, None, :], (QL, JL, KEYS)).reshape(QJ, KEYS)
     ikt[...] = jnp.zeros(ikt.shape, F32)
 
-    def index_part(src):
+    def ship_grads(d):
+        there = peer_s(d)
+        send(rows(diqs, there, QJ), rows(diq_out, me_s, QJ), b_ss.at[d], b_rs.at[d], me_k, there)
+        send(diws.at[there], diwr.at[me_s], v_ss.at[d], v_rs.at[d], me_k, there)
+
+    def index_part(d):
+        src = peer_s(d)
         sim = dot_nt(iqr[src], kb[:, IO:W])
         dl = dlv[...]
         ds = jnp.where(sim > 0, dl * jnp.tile(wv[src], (1, KEYS // 128)), 0.0).astype(BF16)
@@ -532,17 +538,12 @@
         diws[src] = jnp.sum(jnp.where(my_query, dw, 0.0), axis=0)
         diqs[span(src, QJ), :] = dot(ds, kb[:, IO:W])
         ikt[...] += dot(iqt[:, span(src, 128)], ds)
-        pl.when(src == 3)(lambda: ship_home(1))
-        pl.when(src == 6)(lambda: ship_home(2))
+        pl.when(d >= 1)(lambda: ship_grads(d))
+        pl.when(d == 3)(lambda: ship_home(1))
+        pl.when(d == 6)(lambda: ship_home(2))
 
     loop(0, NS, index_part)
 
-    def ship_grads(d):
-        there = peer_s(d)
-        send(rows(diqs, there, QJ), rows(diq_out, me_s, QJ), b_ss.at[d], b_rs.at[d], me_k, there)
-        send(diws.at[there], diwr.at[me_s], v_ss.at[d], v_rs.at[d], me_k, there)
-
-    loop(1, NS, ship_grads)
     diwr[me_s] = diws[me_s]
     here_iq = pltpu.make_async_copy(rows(diqs, me_s, QJ), rows(diq_out, me_s, QJ), fin_sem.at[0])
     here_iq.start()
@@ -594,6 +595,7 @@
     here_iq.wait()
     out_iw.wait()
 
+    out_lat = pltpu.make_async_copy(dlat_v, dlat_out, fin_sem.at[2])
     for g in range(GROUPS):
         loop(1, NK, lambda d: arrived(home_part(orx, g, from_k(d)), o_ss.at[g, d], o_rs.at[g, d]))
         grads = dot(home[...], orx[g, :, 0:WIDTHS[g]])
@@ -601,10 +603,9 @@
             dlat_v[:, :, g * GW:(g + 1) * GW] = grads.reshape(NK, SUB, GW)
         elif g == 2:
             dlat_v[:, :, LAT:KD] = grads[:, 0:KD - LAT].reshape(NK, SUB, KD - LAT)
+            out_lat.start()
         else:
             didx_v[...] = grads.reshape(NK, SUB, ID)
-    out_lat = pltpu.make_async_copy(dlat_v, dlat_out, fin_sem.at[2])
-    out_lat.start()
     out_idx = pltpu.make_async_copy(didx_v, didx_out, fin_sem.at[3])
     out_idx.start()
     for g in range(GROUPS):

time: 95.6 us -> 91.5 us (0.957)
  Pallas kernels: 94.8 us -> 90.6 us
    pallas_call x1, Pallas kernels: 91.8 us -> 87.6 us  [body(): pl.pallas_call(kernel, out_shape=[jax.ShapeDtypeStruct((HL, KD, QT), BF16...]
where the time goes in v7:
time: 91.5 us; the launch traced here: 91.2 us
  Pallas kernels  90.6 us (99%)
    pallas_call x1, Pallas kernels, body(): pl.pallas_call(kernel, out_shape=[jax.ShapeDtypeStruct((HL, KD, QT), BF16...  87.6 us
    pallas_call x1, Pallas kernels, body(): pl.pallas_call(hand_over, out_shape=[jax.ShapeDtypeStruct(o.shape, o.dtyp...  2.96 us

profile of v7, /device:TPU:0, one launch (start us, length us, event | category | flops | bytes accessed | tf_op | source)
XLA Modules:
  0.0 91.2 jit_solution(7364955479904063440)
XLA Ops:
  0.6 87.6 %sparse_attention_backward.1 = (bf16[16,576,128]{2,1,0:T(8,128)(2,1)}, f32[16,16,576]{2,1,0:T(8,128)}, f32[1024,128]{1,0:T(8,128)}, f32[8,128]{1,0:T(8,128)}, f32[16,16,128]{2,1,0:T(8,128)}) custom-call(bf16[16,576,128]{2,1,0:T(8,128)(2,1)} %bitcast.8, bf16[2048,512]{1,0:T(8,128)(2,1)} %bitcast.10, bf16[16,576,128]{2,1,0:T(8,128)(2,1)} %bitcast.9, ...), custom_call_target="tpu_custom_call" | custom-call | tf_op jit(solution)/shard_map/sparse_attention_backward/pallas_call | solution.py:622
  88.3 3.0 %hand_over.1 = (bf16[16,576,128]{2,1,0:T(8,128)(2,1)}, f32[16,16,576]{2,1,0:T(8,128)}, f32[1024,128]{1,0:T(8,128)}, f32[8,128]{1,0:T(8,128)}, f32[16,16,128]{2,1,0:T(8,128)}) custom-call(bf16[16,576,128]{2,1,0:T(8,128)(2,1)} %get-tuple-element.15.refs_0_, f32[16,16,576]{2,1,0:T(8,128)} %get-tuple-element.16.refs_1_, f32[1024,128]{1,0:T(8,128)} %get-tuple-element.17.refs_2_, ...), custom_call_target="tpu_custom_call" | custom-call | tf_op jit(solution)/shard_map/hand_over/pallas_call | solution.py:687
